TPU v7x, 32 devices: a whole 2x2x4 slice. The times are simulated.
32 devices in a mesh: dp: 4 (over y, x), fsdp: 8 (over z, core).
Axes of the slice: x: 2, y: 2, z: 4, core: 2. Of those that a mesh axis runs over, the one named last changes fastest.
Arguments:
- tokens: bfloat16 [8192, 768], P(('dp', 'fsdp')), may hold values from -6 to 6
- memory: bfloat16 [16384, 768], P(('dp', 'fsdp')), may hold values from -6 to 6
- target_lengths: int32 [32], P(('dp', 'fsdp')), may hold values from 1 to 256, as said below
- memory_lengths: int32 [32], P(('dp', 'fsdp')), may hold values from 128 to 512, as said below
- task_ids: int32 [32], P(('dp', 'fsdp')), may hold values from 0 to 7
- cotangent: bfloat16 [8192, 768], P(('dp', 'fsdp')), may hold values from -6 to 6
- self_qkv: bfloat16 [768, 2304], P('fsdp'), may hold values from -0.21875 to 0.21875
- self_out: bfloat16 [768, 768], P('fsdp'), may hold values from -0.875 to 0.875
- cross_q: bfloat16 [768, 768], P('fsdp'), may hold values from -0.21875 to 0.21875
- cross_kv: bfloat16 [768, 1536], P('fsdp'), may hold values from -0.21875 to 0.21875
- cross_out: bfloat16 [768, 768], P('fsdp'), may hold values from -1.25 to 1.25
- ffn_in: bfloat16 [768, 3072], P('fsdp'), may hold values from -0.21875 to 0.21875
- ffn_out: bfloat16 [3072, 768], P('fsdp'), may hold values from -0.109375 to 0.109375
- task_table: float32 [8, 64], replicated, may hold values from -6 to 6
- hyper_in: float32 [64, 128], replicated, may hold values from -0.75 to 0.75
- hyper_gen: bfloat16 [128, 76032], P(None, 'fsdp'), may hold values from -0.5 to 0.5
Outputs:
- mixed_out: bfloat16 [8192, 768], P(('dp', 'fsdp'))
- token_grad: float32 [8192, 768], P(('dp', 'fsdp'))
- memory_grad: float32 [16384, 768], P(('dp', 'fsdp'))
- grad_self_qkv: float32 [768, 2304], P('fsdp')
- grad_self_out: float32 [768, 768], P('fsdp')
- grad_cross_q: float32 [768, 768], P('fsdp')
- grad_cross_kv: float32 [768, 1536], P('fsdp')
- grad_cross_out: float32 [768, 768], P('fsdp')
- grad_ffn_in: float32 [768, 3072], P('fsdp')
- grad_ffn_out: float32 [3072, 768], P('fsdp')
- grad_task_table: float32 [8, 64], replicated
- grad_hyper_in: float32 [64, 128], replicated
- grad_hyper_gen: float32 [128, 76032], P(None, 'fsdp')
Inputs may be any that keep to these rules, and one draw needn't show every extreme that they name: `target_lengths`: sequence s lies in bucket s // 8; bucket b holds lengths from b * 64 + 1 to (b + 1) * 64; some sequence of the last bucket has exactly 256. `memory_lengths`: some sequence has exactly 512.
All inputs are finite; a program needn't handle non-finite values.
Results may differ from a plain program's by a relative error of at most 0.024.
Values may be sent and summed in bfloat16 or wider, within the bound.
No kernel may reach another device: no remote copies, remote signals or barrier semaphores. Data moves between devices by JAX's collectives and lax.ppermute only.
A program may use at most 192 MiB of HBM per device.

v0:
```python
import functools

import jax
import jax.numpy as jnp
from jax import lax
from jax.experimental import pallas as pl
from jax.experimental.pallas import tpu as pltpu
from jax.sharding import PartitionSpec as P

D = 768
HEADS = 12
HEAD = 64
ADAPT = 24
TASKS = 8
BOTH = ("dp", "fsdp")


def matmul(left, right):
    return jnp.dot(left, right, preferred_element_type=jnp.float32)


def matmul_left_t(left, right):
    return lax.dot_general(
        left, right, (((0,), (0,)), ((), ())), preferred_element_type=jnp.float32
    )


def matmul_right_t(left, right):
    return lax.dot_general(
        left, right, (((1,), (1,)), ((), ())), preferred_element_type=jnp.float32
    )


def low(values):
    return values.astype(jnp.bfloat16)


def add_low(left, right):
    return low(left.astype(jnp.float32) + right.astype(jnp.float32))


def rms_factor(values):
    return lax.rsqrt(jnp.mean(values * values, axis=-1, keepdims=True) + 1e-06)


def norm_grad(values, gains, upstream):
    factor = rms_factor(values)
    scaled = upstream * gains
    mean = jnp.mean(values * scaled, axis=-1, keepdims=True)
    part = factor * scaled - values * (factor * factor * factor * mean)
    return part, jnp.sum(upstream * values * factor, axis=0, keepdims=True)


GELU_A = 0.7978845608
GELU_B = 0.044715


def gelu(values):
    inside = GELU_A * (values + GELU_B * values * values * values)
    return 0.5 * values * (1.0 + jnp.tanh(inside))


def gelu_both(values):
    square = values * values
    curve = jnp.tanh(GELU_A * (values + GELU_B * square * values))
    inner = GELU_A * (1.0 + 3.0 * GELU_B * square)
    half = 0.5 * (1.0 + curve)
    return values * half, half + 0.5 * values * (1.0 - curve * curve) * inner


def gelu_slope(values):
    square = values * values
    curve = jnp.tanh(GELU_A * (values + GELU_B * square * values))
    inner = GELU_A * (1.0 + 3.0 * GELU_B * square)
    return 0.5 * (1.0 + curve) + 0.5 * values * (1.0 - curve * curve) * inner


class Group:
    def __init__(self, scalars, refs, scratch, sems, by_block, blocks=(0, 1, 2, 3)):
        self.scalars, self.refs, self.scratch, self.sems = scalars, refs, scratch, sems
        self.by_block, self.blocks = by_block, blocks
        self.staged = len(refs) > 1
        self.waited = False

    def _each(self, act, part=None):
        if not self.staged:
            act(pltpu.make_async_copy(self.refs[0], self.scratch, self.sems.at[0]))
            return
        c = self.scalars[2]
        for place in range(4):
            block = self.which(place)

            def parts(place=place, block=block):
                for side in range(2):
                    source = self.refs[side * 4 + place]
                    if self.by_block and part in (None, place):
                        target = self.scratch.at[place, :, c ^ side]
                        act(pltpu.make_async_copy(source, target, self.sems.at[place * 2 + side]))
                    if not self.by_block:
                        for half in range(2):
                            if part in (None, half):
                                at = pl.ds(half * 2, 2)
                                act(
                                    pltpu.make_async_copy(
                                        source.at[at],
                                        self.scratch.at[at, c ^ side, block],
                                        self.sems.at[(place * 2 + side) * 2 + half],
                                    )
                                )

            if len(self.blocks) == 4:
                parts()
            else:
                wanted = block == self.blocks[0]
                for other in self.blocks[1:]:
                    wanted = wanted | (block == other)
                pl.when(wanted)(parts)

    def start(self):
        self._each(lambda copy: copy.start())

    def wait(self, part=None):
        if self.staged:
            self._each(lambda copy: copy.wait(), part)
        elif not self.waited:
            self._each(lambda copy: copy.wait())
            self.waited = True

    def wait_block(self, index):
        if not self.staged:
            self.wait()
            return
        place, c = self.which(index), self.scalars[2]
        for side in range(2):
            target = self.scratch.at[place, :, c ^ side]
            pltpu.make_async_copy(self.refs[0], target, self.sems.at[place * 2 + side]).wait()

    def place(self, place):
        return self.scratch[place].reshape(D, D)

    def which(self, place):
        return self.scalars[0] ^ place if self.staged else place

    def block(self, index):
        return self.scratch[self.which(index)].reshape(D, D)

    def quarter(self, z):
        return self.scratch[z].reshape(D, D)


def columns_at(block):
    return pl.ds(pl.multiple_of(block * D, D), D)


def part_rows(scalars, value, keep, send, at):
    flat = value.T
    rows = flat.shape[0] // 8
    for parity in range(2):
        here = scalars[2] == parity

        @pl.when(here)
        def _():
            for z in range(4):
                piece = flat[(z * 2 + parity) * rows : (z * 2 + parity + 1) * rows]
                keep[at + z * rows : at + (z + 1) * rows, :] = piece

        @pl.when(jnp.logical_not(here))
        def _():
            for z in range(4):
                piece = flat[(z * 2 + parity) * rows : (z * 2 + parity + 1) * rows]
                send[at + z * rows : at + (z + 1) * rows, :] = piece


class Blocks:
    def __init__(self, scalars, outs, stage, sems):
        self.scalars, self.outs, self.stage, self.sems = scalars, outs, stage, sems
        self.sent = []

    def put(self, block, value):
        rows = value.shape[0] // 4
        value = low(value)
        for z in range(4):
            self.stage[block, z] = value[z * rows : (z + 1) * rows]
        r, c = self.scalars[0] ^ block, self.scalars[2]
        first = jnp.where(c == 0, r % 2, r // 2)
        second = jnp.where(c == 0, r // 2, r % 2)
        for way, out in enumerate(self.outs):
            copy = pltpu.make_async_copy(self.stage.at[block], out.at[second], self.sems.at[block * 2 + way])
            pl.when(first == way)(copy.start)
            self.sent.append((first == way, copy))

    def finish(self):
        for here, copy in self.sent:
            pl.when(here)(copy.wait)


def head_lanes(rows, head):
    lane = lax.broadcasted_iota(jnp.int32, (rows, 128), 1)
    return lane < HEAD if head == 0 else lane >= HEAD


def pick_head(values, head):
    return jnp.where(head_lanes(values.shape[0], head), values, jnp.zeros_like(values))


def pair_at(pair, base=0):
    return pl.ds(pl.multiple_of(base + pair * 128, 128), 128)


def work_on_pairs(first, middle, last, spaces):
    wide, low_spaces = spaces[:2], spaces[2:]
    pairs = HEADS // 2
    first(0, wide[0])

    @pl.loop(0, pairs // 2)
    def _(turn):
        for i in range(2):
            pair = turn * 2 + i
            first(jnp.minimum(pair + 1, pairs - 1), wide[1 - i])
            middle(pair, wide[i], low_spaces[i])
            last(jnp.maximum(pair - 1, 0), low_spaces[1 - i])

    last(pairs - 1, low_spaces[1])


def attend_spaces(keys, queries):
    shape = (2, keys, queries)
    return [(shape, jnp.float32)] * 2 + [(shape, jnp.bfloat16)] * 2


def attend_pairs(q_ref, k_ref, k_at, v_ref, v_at, bias, probs, mixed, spaces):
    ready(q_ref, k_ref, v_ref)
    q_ref, k_ref, v_ref, probs = (inner_of(ref) for ref in (q_ref, k_ref, v_ref, probs))

    def scores_of(pair, wide):
        keys = k_ref[:, pair_at(pair, k_at)]
        for head in range(2):
            wide[head] = matmul_right_t(pick_head(keys, head), q_ref[:, pair_at(pair)])

    def weights_of(pair, wide, space):
        for head in range(2):
            scores = wide[head] + bias
            weights = jnp.exp(scores - jnp.max(scores, axis=0, keepdims=True))
            weights = low(weights * (1.0 / jnp.sum(weights, axis=0, keepdims=True)))
            space[head] = weights
            probs[pair * 2 + head] = weights

    def mix(pair, space):
        values = v_ref[:, pair_at(pair, v_at)].T
        halves = [matmul(values[head * HEAD : (head + 1) * HEAD], space[head]) for head in range(2)]
        mixed[:, pair_at(pair)] = low(jnp.concatenate(halves, axis=0).T)

    work_on_pairs(scores_of, weights_of, mix, spaces)


def attend_pairs_back(
    q_ref, k_ref, k_at, v_ref, v_at, probs, grad_mixed, grad_q, grad_k, gk_at, grad_v, gv_at, spaces
):
    ready(q_ref, k_ref, v_ref, probs)
    q_ref, k_ref, v_ref, probs = (inner_of(ref) for ref in (q_ref, k_ref, v_ref, probs))
    grad_q, grad_k, grad_v = (inner_of(ref) for ref in (grad_q, grad_k, grad_v))

    def grad_weights(pair, wide):
        values = v_ref[:, pair_at(pair, v_at)]
        for head in range(2):
            wide[head] = matmul_right_t(pick_head(values, head), grad_mixed[:, pair_at(pair)])

    def grad_scores(pair, wide, space):
        for head in range(2):
            weights = probs[pair * 2 + head].astype(jnp.float32)
            grads = wide[head]
            total = jnp.sum(grads * weights, axis=0, keepdims=True)
            space[head] = low(weights * (grads - total))

    def products(pair, space):
        queries = q_ref[:, pair_at(pair)]
        keys = k_ref[:, pair_at(pair, k_at)]
        grads = grad_mixed[:, pair_at(pair)]
        keys_t = keys.T
        part_v = [matmul(probs[pair * 2 + head], grads) for head in range(2)]
        part_k = [matmul(space[head], queries) for head in range(2)]
        halves = [matmul(keys_t[head * HEAD : (head + 1) * HEAD], space[head]) for head in range(2)]
        first = head_lanes(keys.shape[0], 0)
        grad_q[:, pair_at(pair)] = low(jnp.concatenate(halves, axis=0).T * HEAD ** (-0.5))
        grad_k[:, pair_at(pair, gk_at)] = low(jnp.where(first, part_k[0], part_k[1]))
        grad_v[:, pair_at(pair, gv_at)] = low(jnp.where(first, part_v[0], part_v[1]))

    work_on_pairs(grad_weights, grad_scores, products, spaces)


def adapter_forward(branch, down, upward):
    inner = matmul(branch, down) * D ** (-0.5)
    active = low(gelu(inner))
    return branch.astype(jnp.float32) + matmul(active, upward) * ADAPT ** (-0.5), inner, active


def adapter_backward(branch, down, upward, inner, active, grad_out):
    grad_low = low(grad_out)
    grad_up = matmul_left_t(active, grad_low) * ADAPT ** (-0.5)
    grad_active = matmul_right_t(grad_low, upward) * ADAPT ** (-0.5)
    grad_inner = low(gelu_slope(inner) * grad_active)
    grad_down = matmul_left_t(branch, grad_inner) * D ** (-0.5)
    grad_branch = low(grad_out + matmul_right_t(grad_inner, down) * D ** (-0.5))
    return grad_branch, grad_down, grad_up


def self_forward_kernel(n, scalars, tokens, gains, down, up, *rest):
    refs, (qkv, probs, branch, inner_out, first_out, normed_cross, *saved, scratch, sems) = rest[: n[0]], rest[n[0] :]
    *halves, normed, mixed = saved[:-4]
    group = Group(scalars, refs, scratch, sems, True)
    fetch(tokens, group)
    inputs = tokens[...].astype(jnp.float32)
    normed[...] = low(inputs * rms_factor(inputs) * gains[0:1])
    rows = inputs.shape[0]
    key = lax.broadcasted_iota(jnp.int32, (rows, rows), 0)
    query = lax.broadcasted_iota(jnp.int32, (rows, rows), 1)
    bias = jnp.where((key <= query) & (key < scalars[3]), 0.0, -1e30)
    if halves:
        part_rows(scalars, normed[...], *halves, 0)
    for b in range(3):
        group.wait_block(b)
        product = matmul(normed[...], group.block(b))
        qkv[:, b * D : (b + 1) * D] = low(product) * (HEAD ** (-0.5) if b == 0 else 1.0)
    send(qkv)
    attend_pairs(qkv, qkv, D, qkv, 2 * D, bias, probs, mixed, saved[-4:])
    send(probs)
    group.wait_block(3)
    branch[...] = low(matmul(mixed[...], group.block(3)))
    adapted, inner, _ = adapter_forward(branch[...], down[...], up[...])
    inner_out[...] = inner
    first = inputs + adapted
    first_out[...] = first
    normed_cross[...] = low(first * rms_factor(first) * gains[1:2])
    send(branch, first_out, normed_cross)
    if halves:
        part_rows(scalars, mixed[...], *halves, D // 2)


def cross_forward_kernel(n, scalars, normed, first, memory, gains, *rest):
    refs, (queries, memory_kv, probs, second_out, normed_ffn, *saved, scratch, sems) = rest[: n[0]], rest[n[0] :]
    *halves, mixed = saved[:-4]
    group = Group(scalars, refs, scratch, sems, True)
    fetch(memory, normed, group, first)
    slot = lax.broadcasted_iota(jnp.int32, (memory.shape[0], 1), 0)
    bias = jnp.where(slot < scalars[4], 0.0, -1e30)
    if halves:
        part_rows(scalars, normed[...], *halves, 0)
        half = memory.shape[0] // 2
        for i in range(2):
            part_rows(scalars, memory[i * half : (i + 1) * half, :], *halves, (2 + i) * (D // 2))
    group.wait()
    queries[...] = low(matmul(normed[...], group.block(0))) * HEAD ** (-0.5)
    for b in range(2):
        memory_kv[:, b * D : (b + 1) * D] = low(matmul(memory[...], group.block(2 + b)))
    send(queries, memory_kv)
    attend_pairs(queries, memory_kv, 0, memory_kv, D, bias, probs, mixed, saved[-4:])
    send(probs)
    second = first[...] + matmul(mixed[...], group.block(1))
    second_out[...] = second
    normed_ffn[...] = low(second * rms_factor(second) * gains[2:3])
    send(second_out, normed_ffn)
    if halves:
        part_rows(scalars, mixed[...], *halves, D // 2)


def ffn_in_kernel(n, scalars, normed, *rest):
    refs, (slope, hidden, *halves, scratch, sems) = rest[: n[0]], rest[n[0] :]
    group = Group(scalars, refs, scratch, sems, True)
    fetch(normed, group)
    if halves:
        part_rows(scalars, normed[...], *halves, 0)
    ahead = None
    for b in range(5):
        product = ahead
        if b < 4:
            group.wait_block(b)
            ahead = matmul(normed[...], group.block(b))
        if b:
            at = slice((b - 1) * D, b * D)
            hidden_b, slope_b = gelu_both(product)
            hidden_b = low(hidden_b)
            slope[:, at] = low(slope_b)
            hidden[:, at] = hidden_b
            send_part(b - 1, slope, hidden)
            if halves:
                flat, half = hidden_b.T, D // 2
                to = slice(b * half, (b + 1) * half)
                even = scalars[2] == 0
                halves[0][to, :] = jnp.where(even, flat[:half], flat[half:])
                halves[1][to, :] = jnp.where(even, flat[half:], flat[:half])


def ffn_out_kernel(n, scalars, hidden, second, cotangent, down, up, *rest):
    refs, (mixed_out, grad_branch, grad_down, grad_up, scratch, sems) = rest[: n[0]], rest[n[0] :]
    group = Group(scalars, refs, scratch, sems, False)
    fetch(hidden, group, second, cotangent)
    rows = hidden.shape[0]
    valid = lax.broadcasted_iota(jnp.int32, (rows, 1), 0) < scalars[3]
    product = None
    for z in range(4):
        if z % 2 == 0:
            group.wait(z // 2)
        term = matmul(hidden[:, z * D : (z + 1) * D], group.quarter(z))
        product = term if product is None else product + term
    branch = low(product)
    adapted, inner, active = adapter_forward(branch, down[...], up[...])
    mixed_out[...] = low(jnp.where(valid, second[...] + adapted, 0.0))
    send(mixed_out)
    grad_result = jnp.where(valid, cotangent[...].astype(jnp.float32), 0.0)
    grad_branch[...], grad_down[...], grad_up[...] = adapter_backward(
        branch, down[...], up[...], inner, active, grad_result
    )


def ffn_back_kernel(n, scalars, grad_branch, slope, *rest):
    refs, (grad_pre, scratch, sems) = rest[: n[0]], rest[n[0] :]
    group = Group(scalars, refs, scratch, sems, False)
    fetch(grad_branch, group, slope)
    for z in range(4):
        if z % 2 == 0:
            group.wait(z // 2)
        at = slice(z * D, (z + 1) * D)
        grad_hidden = matmul_right_t(grad_branch[...], group.quarter(z))
        grad_pre[:, at] = low(slope[:, at].astype(jnp.float32) * grad_hidden)


def cross_views(pack, rows):
    side = pack.at[:, 2 * D :]
    return side.at[:rows], side.at[rows : 2 * rows], pack.at[:, : 2 * D]


def cross_back_kernel(n, scalars, grad_pre, cotangent, second, gains, queries, memory_kv, probs, *rest):
    refs, cross_refs = rest[: n[0]], rest[n[0] : n[0] + n[1]]
    (grad_second_out, grad_gain, pack, grad_mixed, *spaces, scratch, cross_scratch, sems, cross_sems) = rest[n[0] + n[1] :]
    group = Group(scalars, refs, scratch, sems, True)
    cross = Group(scalars, cross_refs, cross_scratch, cross_sems, True, (1,))
    fetch(grad_pre, group)
    rows = second.shape[0]
    valid = lax.broadcasted_iota(jnp.int32, (rows, 1), 0) < scalars[3]
    upstream = None
    for r in range(4):
        group.wait(r)
        if r == 0:
            fetch(second, cotangent, cross)
        if r == 2:
            fetch(queries, memory_kv, probs)
        term = matmul_right_t(grad_pre[:, columns_at(group.which(r))], group.place(r))
        upstream = term if upstream is None else upstream + term
    grad_result = jnp.where(valid, cotangent[...].astype(jnp.float32), 0.0)
    part, grad_gain[...] = norm_grad(second[...], gains[2:3], upstream)
    grad_second = grad_result + part
    grad_second_out[...] = grad_second
    send(grad_second_out)
    grad_cross, grad_q, _ = cross_views(pack, rows)
    grad_cross[...] = low(grad_second)
    cross.wait()
    grad_mixed[...] = low(matmul_right_t(grad_cross[...], cross.block(1)))
    attend_pairs_back(queries, memory_kv, 0, memory_kv, D, probs, grad_mixed, grad_q, pack, 0, pack, D, spaces)


def self_back_kernel(n, scalars, cross_pack, grad_second, first, gains, branch, inner, down, up, qkv, probs, *rest):
    refs, cross_refs = rest[: n[0]], rest[n[0] : n[0] + n[1]]
    (grad_first_out, grad_gain, grad_down, grad_up, pack, grad_mixed, *spaces, scratch, cross_scratch, sems, cross_sems) = rest[n[0] + n[1] :]
    cross = Group(scalars, cross_refs, cross_scratch, cross_sems, True, (0,))
    group = Group(scalars, refs, scratch, sems, True, (3,))
    fetch(cross_pack, cross, first, grad_second, branch, group, qkv, probs)
    _, grad_q, _ = cross_views(cross_pack, first.shape[0])
    cross.wait()
    upstream = matmul_right_t(grad_q[...], cross.block(0))
    part, grad_gain[...] = norm_grad(first[...], gains[1:2], upstream)
    grad_first = grad_second[...] + part
    grad_first_out[...] = grad_first
    send(grad_first_out)
    active = low(gelu(inner[...]))
    grad_branch, grad_down[...], grad_up[...] = adapter_backward(
        branch[...], down[...], up[...], inner[...], active, grad_first
    )
    pack[:, 3 * D :] = grad_branch
    group.wait()
    grad_mixed[...] = low(matmul_right_t(grad_branch, group.block(3)))
    attend_pairs_back(qkv, qkv, D, qkv, 2 * D, probs, grad_mixed, pack, pack, D, pack, 2 * D, spaces)


def rows_product(kept, at, pairs):
    total = None
    for mine, grad in zip(kept, pairs):
        term = matmul(mine[at : at + D // 2, :], grad)
        total = term if total is None else total + term
    return total


def ffn_out_grad_kernel(n, scalars, kept, got, grad, other, *rest):
    *outs, stage, sems = rest
    fetch(kept, grad, got, other)
    blocks = Blocks(scalars, outs, stage, sems)
    rows, half = D // 8, D // 2
    grads = (grad[...], other[...])
    for b in range(4):
        picked = [
            jnp.concatenate([x[(1 + z) * half + b * rows : (1 + z) * half + (b + 1) * rows, :] for z in range(4)])
            for x in (kept, got)
        ]
        blocks.put(b, matmul(picked[0], grads[0]) + matmul(picked[1], grads[1]))
    blocks.finish()


def ffn_in_grad_kernel(n, scalars, kept, got, grad, other, *rest):
    *outs, stage, sems = rest
    fetch(kept, got, grad, other)
    blocks = Blocks(scalars, outs, stage, sems)
    for b in range(4):
        at = slice(b * D, (b + 1) * D)
        grad.ready(b)
        other.ready(b)
        blocks.put(b, rows_product((kept, got), 0, (grad.inner[:, at], other.inner[:, at])))
    blocks.finish()


def cross_grads_kernel(n, scalars, kept, got, pack, other, *rest):
    *outs, stage, sems = rest
    fetch(kept, got, pack, other)
    blocks = Blocks(scalars, outs, stage, sems)
    half = D // 2
    rows = kept.shape[1]
    views = [cross_views(p.inner, rows) for p in (pack, other)]
    ready_part(0, pack, other)
    blocks.put(0, rows_product((kept, got), 0, [v[1][...] for v in views]))
    blocks.put(1, rows_product((kept, got), half, [v[0][...] for v in views]))
    for b in range(2):
        ready_part(1 + b, pack, other)
        at = slice(b * D, (b + 1) * D)
        value = rows_product((kept, got), 2 * half, [v[2][:rows, at] for v in views])
        value += rows_product((kept, got), 3 * half, [v[2][rows:, at] for v in views])
        blocks.put(2 + b, value)
    blocks.finish()


def self_grads_kernel(n, scalars, kept, got, pack, other, *rest):
    *outs, stage, sems = rest
    fetch(kept, got, pack, other)
    blocks = Blocks(scalars, outs, stage, sems)
    for b in range(4):
        at = slice(b * D, (b + 1) * D)
        part = D // 2 if b == 3 else 0
        ready_part(b, pack, other)
        blocks.put(b, rows_product((kept, got), part, (pack.inner[:, at], other.inner[:, at])))
    blocks.finish()


def combine_kernel(slots, scalars, *rest):
    count = sum(len(terms) for terms in slots)
    refs, (out, stage, out_stage, sems, out_sems) = rest[:count], rest[count:]
    copies = []
    for terms in slots:
        for index in terms:
            at = len(copies)
            source = refs[at] if index is None else refs[at].at[index]
            copies.append(pltpu.make_async_copy(source, stage.at[at], sems.at[at]))
    for copy in copies:
        copy.start()
    sent, at = [], 0
    for i, terms in enumerate(slots):
        total = None
        for _ in terms:
            copies[at].wait()
            term = stage[at].astype(jnp.float32)
            total = term if total is None else total + term
            at += 1
        out_stage[i] = low(total)
        target = out if len(slots) == 1 else out.at[:, i]
        sent.append(pltpu.make_async_copy(out_stage.at[i], target, out_sems.at[i]))
        sent[-1].start()
    for copy in sent:
        copy.wait()


def combine(name, scalars, slots):
    slots = [[term if isinstance(term, tuple) else (term, None) for term in terms] for terms in slots]
    flat = [term for terms in slots for term in terms]
    part = flat[0][0].shape[-2:]
    shape = (4,) + ((len(slots),) if len(slots) > 1 else ()) + part
    return pl.pallas_call(
        functools.partial(combine_kernel, [[index for _, index in terms] for terms in slots]),
        out_shape=jax.ShapeDtypeStruct(shape, jnp.bfloat16),
        in_specs=[pl.BlockSpec(memory_space=pltpu.SMEM)]
        + [pl.BlockSpec(memory_space=pltpu.HBM)] * len(flat),
        out_specs=pl.BlockSpec(memory_space=pltpu.HBM),
        scratch_shapes=[
            pltpu.VMEM((len(flat), 4) + part, jnp.bfloat16),
            pltpu.VMEM((len(slots), 4) + part, jnp.bfloat16),
            pltpu.SemaphoreType.DMA((len(flat),)),
            pltpu.SemaphoreType.DMA((len(slots),)),
        ],
        compiler_params=pltpu.CompilerParams(vmem_limit_bytes=63 << 20),
        cost_estimate=pl.CostEstimate(flops=1 << 28, bytes_accessed=1 << 18, transcendentals=0),
        name=name,
    )(scalars, *[array for array, _ in flat])


def plain_grads_kernel(n, scalars, left, right, out, sems):
    fetch(left, right)
    out[...] = low(matmul_left_t(left[...], right[...]))


def pick_kernel(counts, scalars, *rest):
    inputs, outs = rest[:7], rest[7 : 7 + len(counts)]
    stage, sems, out_sems = rest[7 + len(counts) :]
    rows = inputs[0].shape[0]
    qkv, sout, cq, ckv, cout, f_in, f_out = inputs

    def columns(ref):
        return [ref.at[:, pl.ds(b * D, D)] for b in range(ref.shape[1] // D)]

    groups = {
        1: columns(qkv) + [sout],
        2: [cq, cout] + columns(ckv),
        3: columns(f_in),
        4: [f_out.at[pl.ds(b * rows, rows)] for b in range(4)],
    }
    used = 0
    loads = []
    for group, many in counts:
        for i in range(many):
            for b in range(4):
                copy = pltpu.make_async_copy(groups[group][b], stage.at[used], sems.at[used])
                pl.when(scalars[0] == (b ^ 3 if i else b))(copy.start)
            loads.append(copy)
            used += 1
    sent = []
    used = 0
    for (group, many), out in zip(counts, outs):
        for i in range(many):
            loads[used].wait()
            for z in range(4):
                target = out.at[z, i] if many > 1 else out.at[z]
                copy = pltpu.make_async_copy(stage.at[used], target, out_sems.at[used * 4 + z])
                copy.start()
                sent.append(copy)
            used += 1
    for copy in sent:
        copy.wait()


def pick(scalars, shards, counts):
    rows = shards[0].shape[0]
    total = sum(many for _, many in counts)
    shapes = [((4,) if many == 1 else (4, many)) + (rows, D) for _, many in counts]
    return pl.pallas_call(
        functools.partial(pick_kernel, counts),
        out_shape=[jax.ShapeDtypeStruct(shape, jnp.bfloat16) for shape in shapes],
        in_specs=[pl.BlockSpec(memory_space=pltpu.SMEM)]
        + [pl.BlockSpec(memory_space=pltpu.HBM)] * len(shards),
        out_specs=[pl.BlockSpec(memory_space=pltpu.HBM)] * len(counts),
        scratch_shapes=[
            pltpu.VMEM((total, rows, D), jnp.bfloat16),
            pltpu.SemaphoreType.DMA((total,)),
            pltpu.SemaphoreType.DMA((total * 4,)),
        ],
        compiler_params=pltpu.CompilerParams(vmem_limit_bytes=63 << 20),
        cost_estimate=pl.CostEstimate(flops=2 << 26, bytes_accessed=2 << 16, transcendentals=0),
        name="pick",
    )(scalars, *shards)


def plain_grads_kernel(n, scalars, left, right, out, sems):
    out[...] = low(matmul_left_t(left[...], right[...]))


def memory_back_kernel(n, scalars, pack, *rest):
    refs, (memory_grad, scratch, sems) = rest[: n[0]], rest[n[0] :]
    group = Group(scalars, refs, scratch, sems, True, (2, 3))
    fetch(pack, group)
    group.wait_block(2)
    product = matmul_right_t(pack[:, :D], group.block(2))
    group.wait_block(3)
    memory_grad[...] = product + matmul_right_t(pack[:, D : 2 * D], group.block(3))


def token_back_kernel(n, scalars, grad_qkv, tokens, grad_first, gains, *rest):
    refs, (token_grad, grad_gain, scratch, sems) = rest[: n[0]], rest[n[0] :]
    group = Group(scalars, refs, scratch, sems, True, (0, 1, 2))
    fetch(grad_qkv, group, tokens, grad_first)
    group.wait_block(0)
    upstream = matmul_right_t(grad_qkv[:, :D], group.block(0))
    for b in range(1, 3):
        group.wait_block(b)
        upstream += matmul_right_t(grad_qkv[:, b * D : (b + 1) * D], group.block(b))
    part, grad_gain[...] = norm_grad(tokens[...].astype(jnp.float32), gains[0:1], upstream)
    token_grad[...] = grad_first[...] + part


def nbytes(shape, kind):
    total = jnp.dtype(kind).itemsize
    for size in shape:
        total *= size
    return total


class Moved:
    def __init__(self, outer, inner, sems, first, windows, is_input):
        self.inner, self.is_input = inner, is_input
        self.copies, self.flying, self.done = [], set(), set()
        for i, window in enumerate(windows):
            pair = (outer, inner)
            if window is not None:
                at = (pl.ds(window[0], window[1]), pl.ds(window[2], window[3]))
                pair = (outer.at[at], inner.at[at])
            self.copies.append(pltpu.make_async_copy(*(pair if is_input else pair[::-1]), sems.at[first + i]))

    def start(self, part=None):
        for i, copy in enumerate(self.copies):
            if part in (None, i) and i not in self.flying:
                copy.start()
                self.flying.add(i)

    def ready(self, part=None):
        if self.is_input:
            self.start()
            for i, copy in enumerate(self.copies):
                if part in (None, i) and i not in self.done:
                    copy.wait()
                    self.done.add(i)
        return self.inner

    def finish(self):
        self.start()
        for i, copy in enumerate(self.copies):
            if i not in self.done:
                copy.wait()

    @property
    def shape(self):
        return self.inner.shape

    @property
    def at(self):
        return self.ready().at

    def __getitem__(self, index):
        return self.ready()[index]

    def __setitem__(self, index, value):
        self.inner[index] = value


def fetch(*things):
    for thing in things:
        if isinstance(thing, (Moved, Group)):
            thing.start()


def send(*arrays):
    for array in arrays:
        if isinstance(array, Moved):
            array.start()


def send_part(part, *arrays):
    for array in arrays:
        if isinstance(array, Moved):
            array.start(part)


def inner_of(array):
    return array.inner if isinstance(array, Moved) else array


def ready(*arrays):
    for array in arrays:
        if isinstance(array, Moved):
            array.ready()


def ready_part(part, *arrays):
    for array in arrays:
        array.ready(part)


def column_blocks(shape):
    return [(0, shape[0], b * D, D) for b in range(shape[1] // D)]


def tiled(shape):
    return shape[-1] % 128 == 0 and shape[-2] % 16 == 0


def run(kernel, name, micros, scalars, arrays, groups, outs, scratch=(), direct=False, cut=None):
    n = tuple(len(group) for group in groups)
    outs, scratch = list(outs), list(scratch)
    windows = [pair[1] if isinstance(pair, tuple) else [None] for pair in arrays]
    arrays = [pair[0] if isinstance(pair, tuple) else pair for pair in arrays]
    ins = [(a.shape, a.dtype) for a in arrays]
    flat = [part for group in groups for part in group]
    moved = [pair for pair in (ins if direct else ins + outs) if tiled(pair[0])]
    rows = D // 8
    shape = (4, 2, 4, rows, D) if name in ("ffn_out", "ffn_back") else (4, 4, 2, rows, D)
    spaces = scratch + [(shape, jnp.bfloat16)] * len(groups)

    def body(scalar_ref, *refs):
        refs = list(refs)
        inputs, pieces = refs[: len(ins)], refs[len(ins) : len(ins) + len(flat)]
        results = refs[len(ins) + len(flat) :][: len(outs)]
        rest = refs[len(ins) + len(flat) + len(outs) :]
        copies, rest = rest[: len(moved)], rest[len(moved) :]
        if moved:
            sems, rest = rest[0], rest[1:]
        used, first = 0, 0
        for side, pairs in ((inputs, ins), (results, [] if direct else outs)):
            for i, (shape, _) in enumerate(pairs):
                if tiled(shape):
                    parts = windows[i] if side is inputs else (cut or {}).get(i, [None])
                    side[i] = Moved(side[i], copies[used], sems, first, parts, side is inputs)
                    used, first = used + 1, first + len(parts)
        kernel(n, scalar_ref, *inputs, *pieces, *results, *rest)
        for array in inputs + results:
            if isinstance(array, Moved):
                array.finish()

    def spec(shape):
        return pl.BlockSpec(memory_space=pltpu.HBM if tiled(shape) else pltpu.VMEM)

    return pl.pallas_call(
        body,
        out_shape=[jax.ShapeDtypeStruct(shape, kind) for shape, kind in outs],
        in_specs=[pl.BlockSpec(memory_space=pltpu.SMEM)]
        + [spec(shape) for shape, _ in ins]
        + [pl.BlockSpec(memory_space=pltpu.HBM)] * len(flat),
        out_specs=[spec(shape) for shape, _ in outs],
        scratch_shapes=[pltpu.VMEM(shape, kind) for shape, kind in moved]
        + ([pltpu.SemaphoreType.DMA((len(outs) * 4 + sum(map(len, windows)),))] if moved else [])
        + [pltpu.VMEM(shape, kind) for shape, kind in spaces]
        + [pltpu.SemaphoreType.DMA((32,)) for _ in (groups or [None])],
        compiler_params=pltpu.CompilerParams(vmem_limit_bytes=63 << 20),
        cost_estimate=pl.CostEstimate(
            flops=int(micros * 2e8), bytes_accessed=int(micros * 2e5), transcendentals=0
        ),
        name=name,
    )(scalars, *arrays, *flat)


def moves(step):
    pairs = []
    for y in range(2):
        for x in range(2):
            for z in range(4):
                for c in range(2):
                    ty, tx, tz, tc = step(y, x, z, c)
                    pairs.append((((y * 2 + x) * 4 + z) * 2 + c, ((ty * 2 + tx) * 4 + tz) * 2 + tc))
    return pairs


def swap_x(values):
    return lax.ppermute(values, BOTH, moves(lambda y, x, z, c: (y, 1 - x, z, c)))


def swap_y(values):
    return lax.ppermute(values, BOTH, moves(lambda y, x, z, c: (1 - y, x, z, c)))


def swap_core(values):
    return lax.ppermute(values, BOTH, moves(lambda y, x, z, c: (y, x, z, 1 - c)))


def turn_z(values, by):
    return lax.ppermute(values, BOTH, moves(lambda y, x, z, c: (y, x, (z + by) % 4, c)))


def after(value, *marks):
    return lax.optimization_barrier((value,) + marks)[0]


def first_swap(values):
    return lax.ppermute(
        values, BOTH, moves(lambda y, x, z, c: (y, 1 - x, z, c) if c == 0 else (1 - y, x, z, c))
    )


def second_swap(values):
    return lax.ppermute(
        values, BOTH, moves(lambda y, x, z, c: (1 - y, x, z, c) if c == 0 else (y, 1 - x, z, c))
    )


LINES = [[z * 2 + c for z in range(4)] for c in range(2)]


def spread_z(values):
    return lax.all_to_all(
        values, "fsdp", split_axis=0, concat_axis=0, tiled=True, axis_index_groups=LINES
    )


class Layer:
    def __init__(self, scalars, tokens, memory, cotangent, staged):
        self.scalars, self.tokens, self.memory, self.cotangent = scalars, tokens, memory, cotangent
        self.staged = staged
        self.t, self.m = tokens.shape[0], memory.shape[0]

    def hold(self, *marks):
        self.scalars = after(self.scalars, *marks)

    def adapters(self, generated):
        block, start = D * ADAPT, 3 * D
        self.gains = 1.0 + 0.25 * generated[:start].astype(jnp.float32).reshape(3, D)
        self.down_1 = generated[start : start + block].reshape(D, ADAPT)
        self.up_1 = generated[start + block : start + 2 * block].reshape(ADAPT, D)
        self.down_2 = generated[start + 2 * block : start + 3 * block].reshape(D, ADAPT)
        self.up_2 = generated[start + 3 * block : start + 4 * block].reshape(ADAPT, D)

    def rows(self, width=D, kind=jnp.bfloat16):
        return ((self.t, width), kind)

    def wide(self, width=D):
        return self.rows(width, jnp.float32)

    def halves(self, count):
        return [((count * (D // 2), self.t), jnp.bfloat16)] * 2

    def self_forward(self, w1):
        local = [self.rows(), self.rows()]
        outs = run(
            self_forward_kernel,
            "self_forward",
            11,
            self.scalars,
            [self.tokens, self.gains, self.down_1, self.up_1],
            [w1],
            [
                self.rows(3 * D),
                ((HEADS, self.t, self.t), jnp.bfloat16),
                self.rows(),
                self.wide(ADAPT),
                self.wide(),
                self.rows(),
            ]
            + (self.halves(2) if self.staged else local),
            scratch=(local if self.staged else []) + attend_spaces(self.t, self.t),
        )
        self.qkv, self.probs_1, self.branch_1, self.inner_1, self.first, self.normed_2 = outs[:6]
        self.saved_1 = outs[6:]

    def cross_forward(self, w2):
        local = [self.rows()]
        outs = run(
            cross_forward_kernel,
            "cross_forward",
            15,
            self.scalars,
            [self.normed_2, self.first, self.memory, self.gains],
            [w2],
            [
                self.rows(),
                ((self.m, 2 * D), jnp.bfloat16),
                ((HEADS, self.m, self.t), jnp.bfloat16),
                self.wide(),
                self.rows(),
            ]
            + (self.halves(4) if self.staged else local),
            scratch=(local if self.staged else []) + attend_spaces(self.m, self.t),
        )
        self.queries, self.memory_kv, self.probs_2, self.second, self.normed_3 = outs[:5]
        self.saved_2 = outs[5:]

    def ffn_in(self, w3):
        outs = run(
            ffn_in_kernel,
            "ffn_in",
            6,
            self.scalars,
            [self.normed_3],
            [w3],
            [self.rows(4 * D), self.rows(4 * D)] + (self.halves(5) if self.staged else []),
            cut={i: column_blocks((self.t, 4 * D)) for i in range(2)},
        )
        self.slope, self.hidden = outs[:2]
        self.saved_3 = outs[2:]

    def adapter_outs(self):
        return [((D, ADAPT), jnp.float32), ((ADAPT, D), jnp.float32)]

    def ffn_out(self, w4):
        self.mixed_out, self.grad_branch, self.grad_down_2, self.grad_up_2 = run(
            ffn_out_kernel,
            "ffn_out",
            8,
            self.scalars,
            [self.hidden, self.second, self.cotangent, self.down_2, self.up_2],
            [w4],
            [self.rows(), self.rows()] + self.adapter_outs(),
        )

    def ffn_back(self, w4):
        (self.grad_pre,) = run(
            ffn_back_kernel,
            "ffn_back",
            8,
            self.scalars,
            [self.grad_branch, self.slope],
            [w4],
            [self.rows(4 * D)],
        )

    def cross_back(self, w3, w2):
        self.grad_second, self.grad_gain_3, self.cross_pack = run(
            cross_back_kernel,
            "cross_back",
            15,
            self.scalars,
            [
                self.grad_pre,
                self.cotangent,
                self.second,
                self.gains,
                self.queries,
                self.memory_kv,
                self.probs_2,
            ],
            [w3, w2],
            [self.wide(), ((1, D), jnp.float32), ((self.m, 3 * D), jnp.bfloat16)],
            scratch=[self.rows()] + attend_spaces(self.m, self.t),
        )

    def self_back(self, w1, w2):
        self.grad_first, self.grad_gain_2, self.grad_down_1, self.grad_up_1, self.self_pack = run(
            self_back_kernel,
            "self_back",
            0.5,
            self.scalars,
            [
                (self.cross_pack, [(self.t, self.t, 2 * D, D)]),
                self.grad_second,
                self.first,
                self.gains,
                self.branch_1,
                self.inner_1,
                self.down_1,
                self.up_1,
                self.qkv,
                self.probs_1,
            ],
            [w1, w2],
            [self.wide(), ((1, D), jnp.float32)] + self.adapter_outs() + [self.rows(4 * D)],
            scratch=[self.rows()] + attend_spaces(self.t, self.t),
        )

    def token_back(self, w1):
        self.token_grad, self.grad_gain_1 = run(
            token_back_kernel,
            "token_back",
            5,
            self.scalars,
            [(self.self_pack, [(0, self.t, 0, 3 * D)]), self.tokens, self.grad_first, self.gains],
            [w1],
            [self.wide(), ((1, D), jnp.float32)],
        )

    def memory_back(self, w2):
        (self.memory_grad,) = run(
            memory_back_kernel,
            "memory_back",
            0.3,
            self.scalars,
            [(self.cross_pack, [(0, self.m, 0, 2 * D)])],
            [w2],
            [((self.m, D), jnp.float32)],
        )

    def block_grads(self, kernel, name, kept, got, grad, other, windows=None, rows=None):
        stage = ((4, 4, D // 8, D), jnp.bfloat16)
        part = ((2, 4, D // 8, D), jnp.bfloat16)
        if rows:
            kept, got = (kept, [rows + (0, self.t)]), (got, [rows + (0, self.t)])
        if windows:
            grad, other = (grad, windows), (other, windows)
        return run(
            kernel, name, 5, self.scalars, [kept, got, grad, other], [], [part, part], [stage], direct=True
        )

    def plain_grads(self, left, right):
        (out,) = run(
            plain_grads_kernel,
            "plain_grads",
            5,
            self.scalars,
            [left, right],
            [],
            [((left.shape[1], right.shape[1]), jnp.bfloat16)],
        )
        return out

    def grad_generated(self):
        return low(
            jnp.concatenate(
                [
                    0.25 * self.grad_gain_1,
                    0.25 * self.grad_gain_2,
                    0.25 * self.grad_gain_3,
                    self.grad_down_1.reshape(ADAPT, D),
                    self.grad_up_1,
                    self.grad_down_2.reshape(ADAPT, D),
                    self.grad_up_2,
                ]
            )
        ).reshape(-1)


def staged_layer(layer, where, task_ids, hidden_all, hyper_gen, shards):
    q, z, c = where[0], where[1], where[2]

    own_1, own_2, own_3, own_4 = pick(where, shards, [(1, 1), (2, 1), (3, 2), (4, 2)])
    column_1 = spread_z(own_1)
    ids = jnp.stack([task_ids, swap_core(task_ids)])
    ids_ahead = [ids] + [turn_z(ids, 4 - k) for k in (1, 2, 3)]
    gen_shard = low(matmul(hidden_all, hyper_gen))
    column_1 = after(column_1, *ids_ahead)
    near_x_1, near_y_1 = swap_x(column_1), swap_y(column_1)

    column_2 = spread_z(after(own_2, column_1))

    def pick_near(near_x, near_y, *marks):
        return jnp.where(c == 0, after(near_x, *marks), after(near_y, *marks))

    leaving_1 = pick_near(near_x_1, near_y_1)
    far_1 = second_swap(leaving_1)

    def rows_of(tasks):
        select = low(tasks[:, 0:1] == jnp.arange(TASKS, dtype=jnp.int32)[None, :])
        return after(low(matmul(select, gen_shard)), near_x_1, near_y_1, leaving_1, column_2)

    asked = [rows_of(tasks) for tasks in ids_ahead]
    turned = [turn_z(asked[k], k) for k in (1, 2, 3)]
    got = jnp.stack([asked[0]] + turned, axis=1)
    pieces = jnp.concatenate([got[0], swap_core(got[1])])
    slots = jnp.arange(8, dtype=jnp.int32)
    source = ((slots % 2) ^ c) * 4 + (z - slots // 2 + 4) % 4
    unturn = low(source[:, None] == slots[None, :])
    layer.adapters(low(matmul(unturn, pieces)).reshape(-1))

    w1 = [column_1, near_x_1, near_y_1, far_1]
    w1 += [swap_core(after(part, near_x_1)) for part in w1]

    def split(pair, *marks):
        return after(pair, *marks)[:, 0], pair[:, 1]

    def with_other(parts, *marks):
        return parts + [swap_core(after(part, *marks)) for part in parts]

    near_2 = [swap_x(column_2), swap_y(column_2)]
    pair_3 = spread_z(after(own_3, *turned))
    layer.hold(column_2)
    layer.self_forward(w1)
    leaving_2 = pick_near(*near_2, layer.normed_2)
    far_2 = second_swap(leaving_2)
    got_1 = swap_core(after(layer.saved_1[1], leaving_2))
    column_3, far_3 = split(pair_3, leaving_2)
    w2 = [column_2] + near_2 + [far_2]
    w2 += [swap_core(after(part, leaving_2)) for part in w2[:3]] + [swap_core(after(far_2, column_3))]
    near_3 = [swap_x(column_3), swap_y(column_3)]
    pair_4 = spread_z(after(own_4, column_3))
    layer.hold(got_1, column_3)
    layer.cross_forward(w2)
    layer.hold(layer.normed_3)
    w3 = with_other([column_3] + near_3 + [far_3], layer.normed_3, *near_3)
    got_2 = swap_core(after(layer.saved_2[1], *near_3))
    column_4, far_4 = split(pair_4, *near_3)
    layer.hold(got_2, column_4)
    layer.ffn_in(w3)
    near_4 = [swap_x(column_4), swap_y(column_4)]
    got_3 = swap_core(layer.saved_3[1])
    w4 = with_other([column_4] + near_4 + [far_4], layer.hidden)
    layer.hold(got_3)
    layer.ffn_out(w4)

    def first_way(sums, *marks):
        home, away = sums
        return home, first_swap(after(away, *marks))

    def leaving(*sums):
        return combine("leaving", layer.scalars, [[(home, 1), (got, 1)] for home, got in sums])

    def staying(*sums):
        return combine("staying", layer.scalars, [[(home, 0), (got, 0), part] for home, got, part in sums])

    def grads(kernel, name, kept, got, grad, other):
        windows = column_blocks(grad.shape) if grad.shape[1] > D else None
        if kernel is cross_grads_kernel:
            windows = [windows[2]] + windows[:2]
        half = D // 2
        rows = {ffn_in_grad_kernel: (0, half), ffn_out_grad_kernel: (half, 4 * half)}.get(kernel)
        return layer.block_grads(kernel, name, kept, got, grad, other, windows, rows)

    other = swap_core(layer.grad_branch)
    layer.ffn_back(w4)
    other_pre = swap_core(layer.grad_pre)
    layer.cross_back(w3, w2)
    layer.hold(layer.cross_pack)
    g4 = grads(
        ffn_out_grad_kernel, "ffn_out_grad", layer.saved_3[0], got_3, layer.grad_branch, other
    )
    s4 = first_way(g4)
    other = swap_core(after(layer.cross_pack, g4[0]))
    layer.hold(g4[0])
    g3 = grads(
        ffn_in_grad_kernel, "ffn_in_grad", layer.saved_3[0], got_3, layer.grad_pre, other_pre
    )
    s3 = first_way(g3)
    layer.hold(g3[0])
    layer.self_back(w1, w2)
    layer.hold(layer.self_pack)
    t43 = leaving(s4, s3)
    q43 = second_swap(t43)
    other_self = swap_core(after(layer.self_pack, t43))
    layer.hold(t43)
    g2 = grads(
        cross_grads_kernel, "cross_grads", layer.saved_2[0], got_2, layer.cross_pack, other
    )
    s2 = first_way(g2)
    layer.hold(g2[0])
    g1 = grads(
        self_grads_kernel, "self_grads", layer.saved_1[0], got_1, layer.self_pack, other_self
    )
    s1 = first_way(g1)
    layer.hold(g1[0])
    u43 = staying(s4 + ((q43, (slice(None), 0)),), s3 + ((q43, (slice(None), 1)),))
    sent_43 = spread_z(u43)
    layer.hold(u43)
    layer.token_back(w1)
    layer.hold(layer.token_grad)
    t2 = leaving(s2)
    q2 = second_swap(t2)
    layer.hold(t2)
    layer.memory_back(w2)
    layer.hold(layer.memory_grad)
    t1 = leaving(s1)
    q1 = second_swap(t1)
    layer.hold(t1, sent_43)
    own_4, own_3 = jnp.sum(after(sent_43, t1).astype(jnp.float32), axis=0)
    u21 = staying(s2 + (q2,), s1 + (q1,))
    sent_21 = spread_z(u21)

    pieces = after(layer.grad_generated().reshape(4, 2, -1), u21)
    mine = lax.dynamic_index_in_dim(pieces, c, 1, keepdims=False)
    theirs = lax.dynamic_index_in_dim(pieces, 1 - c, 1, keepdims=False)
    both = jnp.stack([mine, swap_core(theirs)], axis=1)
    both = lax.dynamic_slice_in_dim(jnp.concatenate([both, both]), z, 4, 0)
    terms = jnp.concatenate([both[0]] + [turn_z(both[k], k) for k in (1, 2, 3)])
    ids = jnp.concatenate([ids_ahead[(4 - k) % 4] for k in range(4)])[:, 0]
    select = low(jnp.arange(TASKS, dtype=jnp.int32)[:, None] == ids[None, :])
    task_grad = low(matmul(select, terms))
    task_grad = add_low(task_grad, swap_x(task_grad))
    task_grad = task_grad.astype(jnp.float32) + swap_y(task_grad).astype(jnp.float32)

    def sum_owners(part):
        part = part + swap_core(part)
        got = [part] + [turn_z(part, k) for k in (1, 2, 3)]
        return (got[0] + got[2]) + (got[1] + got[3])

    def share(owns):
        own = low(jnp.stack(owns))
        pair = jnp.stack([own, first_swap(own)])
        quad = jnp.concatenate([pair, second_swap(pair)])
        slots = [jnp.where(c == 0, q ^ b, ((q ^ b) % 2) * 2 + (q ^ b) // 2) for b in range(4)]
        return [
            [lax.dynamic_index_in_dim(quad, at, 0, keepdims=False)[i].astype(jnp.float32) for at in slots]
            for i in range(len(owns))
        ]

    own_2, own_1 = jnp.sum(sent_21.astype(jnp.float32), axis=0)
    g3, g4 = share([own_3, own_4])
    g2, g1 = share([own_2, own_1])
    summed = (
        jnp.concatenate(g1[:3], axis=1),
        g1[3],
        g2[0],
        jnp.concatenate(g2[2:], axis=1),
        g2[1],
        jnp.concatenate(g3, axis=1),
        jnp.concatenate(g4, axis=0),
    )
    return summed, task_grad, sum_owners


def plain_layer(layer, task_ids, hidden_all, hyper_gen, groups):
    owners = lax.axis_size("fsdp")

    def whole(shard):
        return lax.all_gather(shard, "fsdp", axis=0, tiled=True)

    w1, w2, w3 = (
        [jnp.concatenate([whole(block) for block in blocks]).reshape(4, 4, 2, D // 8, D)] for blocks in groups[:3]
    )
    w4 = [whole(jnp.concatenate(groups[3])).reshape(4, 2, 4, D // 8, D)]
    select = low(task_ids[:, None] == jnp.arange(TASKS, dtype=jnp.int32)[None, :])
    gen_shard = low(matmul(hidden_all, hyper_gen))
    gen_tasks = lax.all_gather(gen_shard, "fsdp", axis=1, tiled=True)
    layer.adapters(low(matmul(select, gen_tasks)[0]))
    layer.self_forward(w1)
    layer.cross_forward(w2)
    layer.ffn_in(w3)
    layer.ffn_out(w4)
    layer.ffn_back(w4)
    layer.cross_back(w3, w2)
    layer.self_back(w1, w2)
    layer.token_back(w1)
    layer.memory_back(w2)

    def owned(left, right):
        part = low(lax.psum_scatter(layer.plain_grads(left, right), "fsdp", scatter_dimension=0, tiled=True))
        return lax.psum(part, "dp").astype(jnp.float32)

    t = layer.t
    pack = layer.cross_pack
    summed = (
        owned(layer.saved_1[0], layer.self_pack[:, : 3 * D]),
        owned(layer.saved_1[1], layer.self_pack[:, 3 * D :]),
        owned(layer.normed_2, pack[t : 2 * t, 2 * D :]),
        owned(layer.memory, pack[:, : 2 * D]),
        owned(layer.saved_2[0], pack[:t, 2 * D :]),
        owned(layer.normed_3, layer.grad_pre),
        owned(layer.hidden, layer.grad_branch),
    )
    pieces = layer.grad_generated().reshape(owners, 1, -1)
    select = low(jnp.arange(TASKS, dtype=jnp.int32)[:, None] == task_ids[None, :])
    terms = low(select[None].astype(jnp.float32) * pieces.astype(jnp.float32))
    terms = lax.all_to_all(terms, "fsdp", split_axis=0, concat_axis=0, tiled=True)
    task_grad = low(jnp.sum(terms.astype(jnp.float32), axis=0))
    task_grad = lax.psum(task_grad, "dp").astype(jnp.float32)
    return summed, task_grad, lambda part: lax.psum(part, "fsdp")


def hyper_tail(task_grad, pre_all, hidden_all, task_table, hyper_in, hyper_gen, sum_owners):
    grad_hyper_gen = jnp.dot(
        hidden_all.astype(jnp.float32).T, task_grad, precision=lax.Precision.HIGHEST
    )
    grad_hidden = jnp.dot(
        task_grad, hyper_gen.astype(jnp.float32).T, precision=lax.Precision.HIGHEST
    )
    grad_pre_all = gelu_slope(pre_all) * sum_owners(grad_hidden)
    grad_table = jnp.dot(grad_pre_all, hyper_in.T, precision=lax.Precision.HIGHEST)
    grad_first = jnp.dot(task_table.T, grad_pre_all, precision=lax.Precision.HIGHEST)
    return grad_table, grad_first, grad_hyper_gen


def shards(
    tokens,
    memory,
    target_lengths,
    memory_lengths,
    task_ids,
    cotangent,
    self_qkv,
    self_out,
    cross_q,
    cross_kv,
    cross_out,
    ffn_in,
    ffn_out,
    task_table,
    hyper_in,
    hyper_gen,
):
    staged = lax.axis_size("fsdp") == 8 and lax.axis_size("dp") == 4
    pre_all = jnp.dot(task_table, hyper_in, precision=lax.Precision.HIGHEST)
    hidden_all = low(jax.nn.gelu(pre_all))

    def columns(shard):
        return [shard[:, b * D : (b + 1) * D] for b in range(shard.shape[1] // D)]

    q = lax.axis_index("dp").astype(jnp.int32)
    f = lax.axis_index("fsdp").astype(jnp.int32)
    where = jnp.stack([q, f // 2, f % 2])
    scalars = jnp.concatenate([where, target_lengths, memory_lengths])
    layer = Layer(scalars, tokens, memory, cotangent, staged)
    if staged:
        summed, task_grad, sum_owners = staged_layer(
            layer,
            where,
            task_ids,
            hidden_all,
            hyper_gen,
            (self_qkv, self_out, cross_q, cross_kv, cross_out, ffn_in, ffn_out),
        )
    else:
        rows = self_qkv.shape[0]
        groups = (
            columns(self_qkv) + [self_out],
            [cross_q, cross_out] + columns(cross_kv),
            columns(ffn_in),
            [ffn_out[b * rows : (b + 1) * rows] for b in range(4)],
        )
        summed, task_grad, sum_owners = plain_layer(layer, task_ids, hidden_all, hyper_gen, groups)
    grad_table, grad_first, grad_hyper_gen = hyper_tail(
        task_grad, pre_all, hidden_all, task_table, hyper_in, hyper_gen, sum_owners
    )
    return (
        (layer.mixed_out, layer.token_grad, layer.memory_grad)
        + summed
        + (grad_table, grad_first, grad_hyper_gen)
    )


def solution(mesh):
    by_both = P(("dp", "fsdp"), None)
    by_rows = P("fsdp", None)
    return jax.shard_map(
        shards,
        mesh=mesh,
        in_specs=(by_both, by_both)
        + (P(("dp", "fsdp")),) * 3
        + (by_both,)
        + (by_rows,) * 7
        + (P(), P(), P(None, "fsdp")),
        out_specs=(by_both,) * 3 + (by_rows,) * 7 + (P(), P(), P(None, "fsdp")),
        check_vma=False,
    )
```

profile of v0, /device:TPU:0, one launch (start us, length us, event | category | flops | bytes accessed | tf_op | source)
XLA Modules:
  0.0 344.3 jit_solution(12351763822516643552)
XLA Ops:
  1.3 3.6 %pick.1 = (bf16[4,96,768]{2,1,0:T(8,128)(2,1)}, bf16[4,96,768]{2,1,0:T(8,128)(2,1)}, bf16[4,2,96,768]{3,2,1,0:T(8,128)(2,1)}, bf16[4,2,96,768]{3,2,1,0:T(8,128)(2,1)}) custom-call(s32[3]{0:T(128)} %pad_add_fusion.scalars, bf16[96,2304]{1,0:T(8,128)(2,1)} %rest_0_.1, bf16[96,768]{1,0:T(8,128)(2,1)} %rest_1_.1, bf16[96,768]{1,0:T(8,128)(2,1)} %rest_2_.1, ...), custom_call_target="tpu_custom_call" | custom-call | flops 134217728 | bytes 131072 | tf_op jit(solution)/shard_map/pick/pallas_call | solution.py:648
  4.9 6.3 %all-to-all-start = ((bf16[4,96,768]{2,1,0:T(8,128)(2,1)}), bf16[4,96,768]{2,1,0:T(8,128)(2,1)S(1)}, u32[]{:S(2)}, u32[]{:S(2)}) async-start(bf16[4,96,768]{2,1,0:T(8,128)(2,1)} %get-tuple-element.110), calls=%async_computation | async-start | bytes 1179648 | tf_op jit(solution)/shard_map/all_to_all | solution.py:888
  34.5 7.0 %collective-permute-done.5.refs_6_.refs_12_ = bf16[4,96,768]{2,1,0:T(8,128)(2,1)S(1)} collective-permute-done((bf16[4,96,768]{2,1,0:T(8,128)(2,1)S(1)}, bf16[4,96,768]{2,1,0:T(8,128)(2,1)S(1)}, u32[]{:S(2)}, u32[]{:S(2)}) %collective-permute-start.5) | collective-permute-done | bytes 589856 | tf_op jit(solution)/shard_map/ppermute | solution.py:857
  43.7 4.8 %all-to-all-done.1.refs_4_.refs_15_.refs_18_.refs_1_ = bf16[4,96,768]{2,1,0:T(8,128)(2,1)S(1)} async-done(((bf16[4,96,768]{2,1,0:T(8,128)(2,1)}), bf16[4,96,768]{2,1,0:T(8,128)(2,1)S(1)}, u32[]{:S(2)}, u32[]{:S(2)}) %all-to-all-start.1) | async-done | bytes 589856 | tf_op jit(solution)/shard_map/all_to_all | solution.py:888
  54.9 4.5 %all-to-all-start.2 = ((bf16[4,2,96,768]{3,2,1,0:T(8,128)(2,1)}), bf16[4,2,96,768]{3,2,1,0:T(8,128)(2,1)}, u32[]{:S(2)}, u32[]{:S(2)}) async-start(bf16[4,2,96,768]{3,2,1,0:T(8,128)(2,1)} %get-tuple-element.128), calls=%async_computation.2 | async-start | bytes 2359296 | tf_op jit(solution)/shard_map/all_to_all | solution.py:888
  68.4 10.9 %self_forward.1 = (bf16[256,2304]{1,0:T(8,128)(2,1)}, bf16[12,256,256]{2,1,0:T(8,128)(2,1)}, bf16[256,768]{1,0:T(8,128)(2,1)}, f32[256,24]{1,0:T(8,128)}, f32[25...) custom-call(s32[5]{0:T(128)} %concatenate.61.scalar_ref.scalars, ...), custom_call_target="tpu_custom_call" | custom-call | flops 2200000000 | bytes 2200000 | tf_op jit(solution)/shard_map/self_forward/pallas_call | solution.py:822
  89.0 4.3 %all-to-all-start.3 = ((bf16[4,2,96,768]{3,2,1,0:T(8,128)(2,1)}), bf16[4,2,96,768]{3,2,1,0:T(8,128)(2,1)}, u32[]{:S(2)}, u32[]{:S(2)}) async-start(bf16[4,2,96,768]{3,2,1,0:T(8,128)(2,1)} %get-tuple-element.141), calls=%async_computation.3 | async-start | bytes 2359296 | tf_op jit(solution)/shard_map/all_to_all | solution.py:888
  100.3 24.5 %cross_forward.1 = (bf16[256,768]{1,0:T(8,128)(2,1)}, bf16[512,1536]{1,0:T(8,128)(2,1)}, bf16[12,512,256]{2,1,0:T(8,128)(2,1)}, f32[256,768]{1,0:T(8,128)}, bf16...) custom-call(s32[5]{0:T(128)} %concatenate.61.scalar_ref.scalars, ...), custom_call_target="tpu_custom_call" | custom-call | flops 3000000000 | bytes 3000000 | tf_op jit(solution)/shard_map/cross_forward/pallas_call | solution.py:822
  131.0 8.7 %ffn_in.1 = (bf16[256,3072]{1,0:T(8,128)(2,1)}, bf16[256,3072]{1,0:T(8,128)(2,1)}, bf16[1920,256]{1,0:T(8,128)(2,1)}, bf16[1920,256]{1,0:T(8,128)(2,1)}) custom-call(s32[5]{0:T(128)} %concatenate.61.scalar_ref.scalars, bf16[256,768]{1,0:T(8,128)(2,1)} %get-tuple-element.136.refs_0_, bf16[4,96,768]{2,1,0:T(8,128)(2,1)} %slice_bitcast_fusion.3.refs_1_.refs_7_, ...), custom_call_target="tpu_custom_call" | custom-call | flops 1200000000 | bytes 1200000 | tf_op jit(solution)/shard_map/ffn_in/pallas_call | solution.py:822
  149.4 8.8 %ffn_out.1 = (bf16[256,768]{1,0:T(8,128)(2,1)}, bf16[256,768]{1,0:T(8,128)(2,1)}, f32[768,24]{1,0:T(8,128)}, f32[24,768]{1,0:T(8,128)}) custom-call(s32[5]{0:T(128)} %concatenate.61.scalar_ref.scalars, bf16[256,3072]{1,0:T(8,128)(2,1)} %get-tuple-element.150.refs_0_, f32[256,768]{1,0:T(8,128)} %get-tuple-element.151.refs_1_.refs_2_, ...), custom_call_target="tpu_custom_call" | custom-call | flops 1600000000 | bytes 1600000 | tf_op jit(solution)/shard_map/ffn_out/pallas_call | solution.py:822
  158.2 7.1 %ffn_back.1.refs_0_.refs_2_ = bf16[256,3072]{1,0:T(8,128)(2,1)} custom-call(s32[5]{0:T(128)} %concatenate.61.scalar_ref.scalars, bf16[256,768]{1,0:T(8,128)(2,1)} %get-tuple-element.157.refs_0_.refs_2_, bf16[256,3072]{1,0:T(8,128)(2,1)} %get-tuple-element.158.refs_1_, bf16[4,96,768]{2,1,0:T(8,128)(2,1)} %copy-done.3, ...), custom_call_target="tpu_custom_call" | custom-call | flops 1600000000 | bytes 1600000 | tf_op jit(solution)/shard_map/ffn_back/pallas_call | solution.py:822
  165.9 14.4 %cross_back.1 = (f32[256,768]{1,0:T(8,128)}, f32[1,768]{1,0:T(1,128)}, bf16[512,2304]{1,0:T(8,128)(2,1)}) custom-call(s32[5]{0:T(128)} %concatenate.61.scalar_ref.scalars, bf16[256,3072]{1,0:T(8,128)(2,1)} %ffn_back.1.refs_0_.refs_2_, bf16[256,768]{1,0:T(8,128)(2,1)} %refs_1_.2, f32[256,768]{1,0:T(8,128)} %get-tuple-element.151.refs_1_.refs_2_, ...), custom_call_target="tpu_custom_call" | custom-call | flops 3000000000 | bytes 3000000 | tf_op jit(solution)/shard_map/cross_back/pallas_call | solution.py:822
  180.3 4.9 %ffn_out_grad.1 = (bf16[2,4,96,768]{3,2,1,0:T(8,128)(2,1)}, bf16[2,4,96,768]{3,2,1,0:T(8,128)(2,1)}) custom-call(s32[5]{0:T(128)} %concatenate.61.scalar_ref.scalars, bf16[1920,256]{1,0:T(8,128)(2,1)} %get-tuple-element.164.refs_0_, bf16[1920,256]{1,0:T(8,128)(2,1)} %copy-done.21, bf16[256,768]{1,0:T(8,128)(2,1)} %get-tuple-element.157.refs_0_.refs_2_, ...), custom_call_target="tpu_custom_call" | custom-call | flops 1000000000 | bytes 1000000 | tf_op jit(solution)/shard_map/ffn_out_grad/pallas_call | solution.py:822
  186.0 5.9 %ffn_in_grad.1 = (bf16[2,4,96,768]{3,2,1,0:T(8,128)(2,1)}, bf16[2,4,96,768]{3,2,1,0:T(8,128)(2,1)}) custom-call(s32[5]{0:T(128)} %concatenate.61.scalar_ref.scalars, bf16[1920,256]{1,0:T(8,128)(2,1)} %get-tuple-element.164.refs_0_, bf16[1920,256]{1,0:T(8,128)(2,1)} %copy-done.21, bf16[256,3072]{1,0:T(8,128)(2,1)} %ffn_back.1.refs_0_.refs_2_, ...), custom_call_target="tpu_custom_call" | custom-call | flops 1000000000 | bytes 1000000 | tf_op jit(solution)/shard_map/ffn_in_grad/pallas_call | solution.py:822
  193.3 11.3 %self_back.1 = (f32[256,768]{1,0:T(8,128)}, f32[1,768]{1,0:T(1,128)}, f32[768,24]{1,0:T(8,128)}, f32[24,768]{1,0:T(8,128)}, bf16[256,3072]{1,0:T(8,128)(2,1)}) custom-call(s32[5]{0:T(128)} %concatenate.61.scalar_ref.scalars, bf16[512,2304]{1,0:T(8,128)(2,1)} %get-tuple-element.180.refs_0_.refs_2_, f32[256,768]{1,0:T(8,128)} %get-tuple-element.169.refs_1_, ...), custom_call_target="tpu_custom_call" | custom-call | flops 100000000 | bytes 100000 | tf_op jit(solution)/shard_map/self_back/pallas_call | solution.py:822
  204.7 9.8 %collective-permute-done.40.rest_3_.rest_4_ = bf16[2,4,96,768]{3,2,1,0:T(8,128)(2,1)} collective-permute-done((bf16[2,4,96,768]{3,2,1,0:T(8,128)(2,1)}, bf16[2,4,96,768]{3,2,1,0:T(8,128)(2,1)}, u32[]{:S(2)}, u32[]{:S(2)}) %collective-permute-start.40) | collective-permute-done | bytes 1179680 | tf_op jit(solution)/shard_map/ppermute | solution.py:873
  218.8 7.8 %cross_grads.1 = (bf16[2,4,96,768]{3,2,1,0:T(8,128)(2,1)}, bf16[2,4,96,768]{3,2,1,0:T(8,128)(2,1)}) custom-call(s32[5]{0:T(128)} %concatenate.61.scalar_ref.scalars, bf16[1536,256]{1,0:T(8,128)(2,1)} %get-tuple-element.179.refs_0_, bf16[1536,256]{1,0:T(8,128)(2,1)} %copy-done.22, bf16[512,2304]{1,0:T(8,128)(2,1)} %get-tuple-element.180.refs_0_.refs_2_, ...), custom_call_target="tpu_custom_call" | custom-call | flops 1000000000 | bytes 1000000 | tf_op jit(solution)/shard_map/cross_grads/pallas_call | solution.py:822
  227.5 6.0 %self_grads.1 = (bf16[2,4,96,768]{3,2,1,0:T(8,128)(2,1)}, bf16[2,4,96,768]{3,2,1,0:T(8,128)(2,1)}) custom-call(s32[5]{0:T(128)} %concatenate.61.scalar_ref.scalars, bf16[768,256]{1,0:T(8,128)(2,1)} %get-tuple-element.183.refs_0_, bf16[768,256]{1,0:T(8,128)(2,1)} %copy-done.25, bf16[256,3072]{1,0:T(8,128)(2,1)} %get-tuple-element.184.refs_2_.refs_0_, ...), custom_call_target="tpu_custom_call" | custom-call | flops 1000000000 | bytes 1000000 | tf_op jit(solution)/shard_map/self_grads/pallas_call | solution.py:822
  234.7 4.3 %collective-permute-done.43.rest_2_.rest_5_ = bf16[4,2,96,768]{3,2,1,0:T(8,128)(2,1)} collective-permute-done((bf16[4,2,96,768]{3,2,1,0:T(8,128)(2,1)}, bf16[4,2,96,768]{3,2,1,0:T(8,128)(2,1)}, u32[]{:S(2)}, u32[]{:S(2)}) %collective-permute-start.43) | collective-permute-done | bytes 1179680 | tf_op jit(solution)/shard_map/ppermute | solution.py:879
  239.1 3.6 %staying.2 = bf16[4,2,96,768]{3,2,1,0:T(8,128)(2,1)} custom-call(s32[5]{0:T(128)} %concatenate.61.scalar_ref.scalars, bf16[2,4,96,768]{3,2,1,0:T(8,128)(2,1)} %get-tuple-element.165.rest_0_, bf16[2,4,96,768]{3,2,1,0:T(8,128)(2,1)} %collective-permute-done.39.rest_1_, bf16[4,2,96,768]{3,2,1,0:T(8,128)(2,1)} %collective-permute-done.43.rest_2_.rest_5_, ...), custom_call_target="tpu_custom_call" | custom-call | flops 268435456 | bytes 262144 | tf_op jit(solution)/shard_map/staying/pallas_call | solution.py:582
  242.7 5.4 %all-to-all-start.4 = ((bf16[4,2,96,768]{3,2,1,0:T(8,128)(2,1)}), bf16[4,2,96,768]{3,2,1,0:T(8,128)(2,1)}, u32[]{:S(2)}, u32[]{:S(2)}) async-start(bf16[4,2,96,768]{3,2,1,0:T(8,128)(2,1)} %staying.2), calls=%async_computation.4 | async-start | bytes 2359296 | tf_op jit(solution)/shard_map/all_to_all | solution.py:888
  248.1 6.3 %token_back.1 = (f32[256,768]{1,0:T(8,128)}, f32[1,768]{1,0:T(1,128)}) custom-call(s32[5]{0:T(128)} %concatenate.61.scalar_ref.scalars, bf16[256,3072]{1,0:T(8,128)(2,1)} %get-tuple-element.184.refs_2_.refs_0_, bf16[256,768]{1,0:T(8,128)(2,1)} %refs_1_.3, f32[256,768]{1,0:T(8,128)} %get-tuple-element.188.refs_2_, f32[3,768]{1,0:T(4,128)} %multiply_add_fusion.refs_1_.refs_3_, ...), custom_call_target="tpu_custom_call" | custom-call | flops 1000000000 | bytes 1000000 | tf_op jit(solution)/shard_map/token_back/pallas_call | solution.py:822
  258.7 5.6 %memory_back.1 = f32[512,768]{1,0:T(8,128)} custom-call(s32[5]{0:T(128)} %concatenate.61.scalar_ref.scalars, bf16[512,2304]{1,0:T(8,128)(2,1)} %get-tuple-element.180.refs_0_.refs_2_, bf16[4,96,768]{2,1,0:T(8,128)(2,1)} %copy-done.2, bf16[4,96,768]{2,1,0:T(8,128)(2,1)} %collective-permute-done.15.refs_5_.refs_16_.refs_19_.refs_2_, ...), custom_call_target="tpu_custom_call" | custom-call | flops 60000000 | bytes 60000 | tf_op jit(solution)/shard_map/memory_back/pallas_call | solution.py:822
  270.7 3.9 %all-to-all-done.4 = bf16[4,2,96,768]{3,2,1,0:T(8,128)(2,1)} async-done(((bf16[4,2,96,768]{3,2,1,0:T(8,128)(2,1)}), bf16[4,2,96,768]{3,2,1,0:T(8,128)(2,1)}, u32[]{:S(2)}, u32[]{:S(2)}) %all-to-all-start.4) | async-done | bytes 1179680 | tf_op jit(solution)/shard_map/all_to_all | solution.py:888
  283.4 3.9 %collective-permute-start.55 = (bf16[2,9504]{1,0:T(2,128)(2,1)S(1)}, bf16[2,9504]{1,0:T(2,128)(2,1)S(1)}, u32[]{:S(2)}, u32[]{:S(2)}) collective-permute-start(bf16[2,9504]{1,0:T(2,128)(2,1)S(1)} %bitcast.127), channel_id=1, source_target_pairs={{0,6},{1,7},{2,0},{3,1},{4,2},{5,3},{6,4},{7,5},{8,14},{9,15},{10,... | collective-permute-start | bytes 114056 | tf_op jit(solution)/shard_map/ppermute | solution.py:865
  289.1 4.5 %all-to-all-start.5 = ((bf16[4,2,96,768]{3,2,1,0:T(8,128)(2,1)}), bf16[4,2,96,768]{3,2,1,0:T(8,128)(2,1)}, u32[]{:S(2)}, u32[]{:S(2)}) async-start(bf16[4,2,96,768]{3,2,1,0:T(8,128)(2,1)} %staying.3), calls=%async_computation.5 | async-start | bytes 2359296 | tf_op jit(solution)/shard_map/all_to_all | solution.py:888
  295.7 3.6 %collective-permute-done.56 = bf16[8,9504]{1,0:T(8,128)(2,1)S(1)} collective-permute-done((bf16[8,9504]{1,0:T(8,128)(2,1)S(1)}, bf16[8,9504]{1,0:T(8,128)(2,1)S(1)}, u32[]{:S(2)}, u32[]{:S(2)}) %collective-permute-start.56) | collective-permute-done | bytes 152096 | tf_op jit(solution)/shard_map/ppermute | solution.py:853
  300.9 5.4 %collective-permute-done.57 = bf16[8,9504]{1,0:T(8,128)(2,1)S(1)} collective-permute-done((bf16[8,9504]{1,0:T(8,128)(2,1)S(1)}, bf16[8,9504]{1,0:T(8,128)(2,1)S(1)}, u32[]{:S(2)}, u32[]{:S(2)}) %collective-permute-start.57) | collective-permute-done | bytes 152096 | tf_op jit(solution)/shard_map/ppermute | solution.py:857
  309.3 3.8 %collective-permute-start.61 = (f32[8,128]{1,0:T(8,128)S(1)}, f32[8,128]{1,0:T(8,128)S(1)}, u32[]{:S(2)}, u32[]{:S(2)}) collective-permute-start(f32[8,128]{1,0:T(8,128)S(1)} %add.186), channel_id=1, source_target_pairs={{0,6},{1,7},{2,0},{3,1},{4,2},{5,3},{6,4},{7,5},{8,14},{9,15},{10,... | collective-permute-start | bytes 12296 | tf_op jit(solution)/shard_map/ppermute | solution.py:865
  314.2 5.9 %fusion = f32[128,9504]{0,1:T(8,128)} fusion(bf16[8,9504]{1,0:T(8,128)(2,1)S(1)} %collective-permute-done.57, bf16[8,9504]{1,0:T(8,128)(2,1)S(1)} %add_convert_fusion, f32[8,128]{1,0:T(8,128)S(1)} %fusion.62), kind=kOutput, calls=%fused_computation.32 | convolution fusion | flops 117022464 | bytes 5174272 | tf_op jit(solution)/shard_map/dot_general | solution.py:1332
  325.4 5.7 %collective-permute-done.48 = bf16[2,96,768]{2,1,0:T(8,128)(2,1)S(1)} collective-permute-done((bf16[2,96,768]{2,1,0:T(8,128)(2,1)S(1)}, bf16[2,96,768]{2,1,0:T(8,128)(2,1)S(1)}, u32[]{:S(2)}, u32[]{:S(2)}) %collective-permute-start.48) | collective-permute-done | bytes 294944 | tf_op jit(solution)/shard_map/ppermute | solution.py:873
  334.2 6.9 %collective-permute-done.49 = bf16[2,2,96,768]{3,2,1,0:T(8,128)(2,1)S(1)} collective-permute-done((bf16[2,2,96,768]{3,2,1,0:T(8,128)(2,1)S(1)}, bf16[2,2,96,768]{3,2,1,0:T(8,128)(2,1)S(1)}, u32[]{:S(2)}, u32[]{:S(2)}) %collective-permute-start.49) | collective-permute-done | bytes 589856 | tf_op jit(solution)/shard_map/ppermute | solution.py:879
  (257 shorter events, 121.0 us)
Async XLA Ops:
  4.9 22.3 %all-to-all-start = ((bf16[4,96,768]{2,1,0:T(8,128)(2,1)}), bf16[4,96,768]{2,1,0:T(8,128)(2,1)S(1)}, u32[]{:S(2)}, u32[]{:S(2)}) async-start(bf16[4,96,768]{2,1,0:T(8,128)(2,1)} %get-tuple-element.110), calls=%async_computation | async-start | bytes 1179648 | tf_op jit(solution)/shard_map/all_to_all | solution.py:888
  27.2 14.3 %collective-permute-start.5 = (bf16[4,96,768]{2,1,0:T(8,128)(2,1)S(1)}, bf16[4,96,768]{2,1,0:T(8,128)(2,1)S(1)}, u32[]{:S(2)}, u32[]{:S(2)}) collective-permute-start(bf16[4,96,768]{2,1,0:T(8,128)(2,1)S(1)} %all-to-all-done.refs_4_.refs_10_), channel_id=1, source_target_pairs={{0,16},{1,17},{2,18},{3,19},{4,20},{5,21},{6,22},{7,23},{8,24},{9,... | collective-permute-start | bytes 1769480 | tf_op jit(solution)/shard_map/ppermute | solution.py:857
  28.8 13.9 %collective-permute-start.4 = (bf16[4,96,768]{2,1,0:T(8,128)(2,1)S(1)}, bf16[4,96,768]{2,1,0:T(8,128)(2,1)S(1)}, u32[]{:S(2)}, u32[]{:S(2)}) collective-permute-start(bf16[4,96,768]{2,1,0:T(8,128)(2,1)S(1)} %all-to-all-done.refs_4_.refs_10_), channel_id=1, source_target_pairs={{0,8},{1,9},{2,10},{3,11},{4,12},{5,13},{6,14},{7,15},{8,0},{9,1},... | collective-permute-start | bytes 1769480 | tf_op jit(solution)/shard_map/ppermute | solution.py:853
  30.3 18.2 %all-to-all-start.1 = ((bf16[4,96,768]{2,1,0:T(8,128)(2,1)}), bf16[4,96,768]{2,1,0:T(8,128)(2,1)S(1)}, u32[]{:S(2)}, u32[]{:S(2)}) async-start(bf16[4,96,768]{2,1,0:T(8,128)(2,1)} %get-tuple-element.112), calls=%async_computation.1 | async-start | bytes 1179648 | tf_op jit(solution)/shard_map/all_to_all | solution.py:888
  52.6 11.3 %collective-permute-start.10 = (bf16[4,96,768]{2,1,0:T(8,128)(2,1)}, bf16[4,96,768]{2,1,0:T(8,128)(2,1)S(1)}, u32[]{:S(2)}, u32[]{:S(2)}) collective-permute-start(bf16[4,96,768]{2,1,0:T(8,128)(2,1)} %broadcast_select_fusion.1), channel_id=1, source_target_pairs={{0,16},{1,9},{2,18},{3,11},{4,20},{5,13},{6,22},{7,15},{8,24},{9,1... | collective-permute-start | bytes 1769480 | tf_op jit(solution)/shard_map/ppermute | solution.py:879
  53.2 11.4 %collective-permute-start.11 = (bf16[4,96,768]{2,1,0:T(8,128)(2,1)S(1)}, bf16[4,96,768]{2,1,0:T(8,128)(2,1)}, u32[]{:S(2)}, u32[]{:S(2)}) collective-permute-start(bf16[4,96,768]{2,1,0:T(8,128)(2,1)S(1)} %all-to-all-done.refs_4_.refs_10_), channel_id=1, source_target_pairs={{0,1},{1,0},{2,3},{3,2},{4,5},{5,4},{6,7},{7,6},{8,9},{9,8},{10,11... | collective-permute-start | bytes 1769480 | tf_op jit(solution)/shard_map/ppermute | solution.py:861
  54.9 32.2 %all-to-all-start.2 = ((bf16[4,2,96,768]{3,2,1,0:T(8,128)(2,1)}), bf16[4,2,96,768]{3,2,1,0:T(8,128)(2,1)}, u32[]{:S(2)}, u32[]{:S(2)}) async-start(bf16[4,2,96,768]{3,2,1,0:T(8,128)(2,1)} %get-tuple-element.128), calls=%async_computation.2 | async-start | bytes 2359296 | tf_op jit(solution)/shard_map/all_to_all | solution.py:888
  61.3 18.0 %collective-permute-start.16 = (bf16[4,96,768]{2,1,0:T(8,128)(2,1)S(1)}, bf16[4,96,768]{2,1,0:T(8,128)(2,1)}, u32[]{:S(2)}, u32[]{:S(2)}) collective-permute-start(bf16[4,96,768]{2,1,0:T(8,128)(2,1)S(1)} %all-to-all-done.1.refs_4_.refs_15_.refs_18_.refs_1_), channel_id=1, source_target_pairs={{0,16},{1,17},{2,18},{3,19},{4,20},{5,21},{6,22},{7,23},{8,24},{9,... | collective-permute-start | bytes 1769480 | tf_op jit(solution)/shard_map/ppermute | solution.py:857
  64.6 15.8 %collective-permute-start.15 = (bf16[4,96,768]{2,1,0:T(8,128)(2,1)S(1)}, bf16[4,96,768]{2,1,0:T(8,128)(2,1)}, u32[]{:S(2)}, u32[]{:S(2)}) collective-permute-start(bf16[4,96,768]{2,1,0:T(8,128)(2,1)S(1)} %all-to-all-done.1.refs_4_.refs_15_.refs_18_.refs_1_), channel_id=1, source_target_pairs={{0,8},{1,9},{2,10},{3,11},{4,12},{5,13},{6,14},{7,15},{8,0},{9,1},... | collective-permute-start | bytes 1769480 | tf_op jit(solution)/shard_map/ppermute | solution.py:853
  82.3 12.0 %collective-permute-start.18 = (bf16[4,96,768]{2,1,0:T(8,128)(2,1)}, bf16[4,96,768]{2,1,0:T(8,128)(2,1)S(1)}, u32[]{:S(2)}, u32[]{:S(2)}) collective-permute-start(bf16[4,96,768]{2,1,0:T(8,128)(2,1)} %broadcast_select_fusion), channel_id=1, source_target_pairs={{0,16},{1,9},{2,18},{3,11},{4,20},{5,13},{6,22},{7,15},{8,24},{9,1... | collective-permute-start | bytes 1769480 | tf_op jit(solution)/shard_map/ppermute | solution.py:879
  89.0 38.3 %all-to-all-start.3 = ((bf16[4,2,96,768]{3,2,1,0:T(8,128)(2,1)}), bf16[4,2,96,768]{3,2,1,0:T(8,128)(2,1)}, u32[]{:S(2)}, u32[]{:S(2)}) async-start(bf16[4,2,96,768]{3,2,1,0:T(8,128)(2,1)} %get-tuple-element.141), calls=%async_computation.3 | async-start | bytes 2359296 | tf_op jit(solution)/shard_map/all_to_all | solution.py:888
  96.1 28.7 %collective-permute-start.24 = (bf16[4,96,768]{2,1,0:T(8,128)(2,1)}, bf16[4,96,768]{2,1,0:T(8,128)(2,1)}, u32[]{:S(2)}, u32[]{:S(2)}) collective-permute-start(bf16[4,96,768]{2,1,0:T(8,128)(2,1)} %slice_bitcast_fusion.3.refs_1_.refs_7_), channel_id=1, source_target_pairs={{0,16},{1,17},{2,18},{3,19},{4,20},{5,21},{6,22},{7,23},{8,24},{9,... | collective-permute-start | bytes 1769480 | tf_op jit(solution)/shard_map/ppermute | solution.py:857
  97.7 27.2 %collective-permute-start.23 = (bf16[4,96,768]{2,1,0:T(8,128)(2,1)}, bf16[4,96,768]{2,1,0:T(8,128)(2,1)}, u32[]{:S(2)}, u32[]{:S(2)}) collective-permute-start(bf16[4,96,768]{2,1,0:T(8,128)(2,1)} %slice_bitcast_fusion.3.refs_1_.refs_7_), channel_id=1, source_target_pairs={{0,8},{1,9},{2,10},{3,11},{4,12},{5,13},{6,14},{7,15},{8,0},{9,1},... | collective-permute-start | bytes 1769480 | tf_op jit(solution)/shard_map/ppermute | solution.py:853
  128.4 15.8 %collective-permute-start.32 = (bf16[4,96,768]{2,1,0:T(8,128)(2,1)S(1)}, bf16[4,96,768]{2,1,0:T(8,128)(2,1)}, u32[]{:S(2)}, u32[]{:S(2)}) collective-permute-start(bf16[4,96,768]{2,1,0:T(8,128)(2,1)S(1)} %slice_bitcast_fusion.2.refs_5_.refs_2_), channel_id=1, source_target_pairs={{0,16},{1,17},{2,18},{3,19},{4,20},{5,21},{6,22},{7,23},{8,24},{9,... | collective-permute-start | bytes 1769480 | tf_op jit(solution)/shard_map/ppermute | solution.py:857
  130.0 15.5 %collective-permute-start.31 = (bf16[4,96,768]{2,1,0:T(8,128)(2,1)S(1)}, bf16[4,96,768]{2,1,0:T(8,128)(2,1)}, u32[]{:S(2)}, u32[]{:S(2)}) collective-permute-start(bf16[4,96,768]{2,1,0:T(8,128)(2,1)S(1)} %slice_bitcast_fusion.2.refs_5_.refs_2_), channel_id=1, source_target_pairs={{0,8},{1,9},{2,10},{3,11},{4,12},{5,13},{6,14},{7,15},{8,0},{9,1},... | collective-permute-start | bytes 1769480 | tf_op jit(solution)/shard_map/ppermute | solution.py:853
  165.3 20.7 %collective-permute-start.38 = (bf16[256,3072]{1,0:T(8,128)(2,1)}, bf16[256,3072]{1,0:T(8,128)(2,1)}, u32[]{:S(2)}, u32[]{:S(2)}) collective-permute-start(bf16[256,3072]{1,0:T(8,128)(2,1)} %ffn_back.1.refs_0_.refs_2_), channel_id=1, source_target_pairs={{0,1},{1,0},{2,3},{3,2},{4,5},{5,4},{6,7},{7,6},{8,9},{9,8},{10,11... | collective-permute-start | bytes 4718600 | tf_op jit(solution)/shard_map/ppermute | solution.py:861
  165.5 14.8 %collective-permute-start.37 = (bf16[256,768]{1,0:T(8,128)(2,1)S(1)}, bf16[256,768]{1,0:T(8,128)(2,1)}, u32[]{:S(2)}, u32[]{:S(2)}) collective-permute-start(bf16[256,768]{1,0:T(8,128)(2,1)S(1)} %copy-done.24), channel_id=1, source_target_pairs={{0,1},{1,0},{2,3},{3,2},{4,5},{5,4},{6,7},{7,6},{8,9},{9,8},{10,11... | collective-permute-start | bytes 1179656 | tf_op jit(solution)/shard_map/ppermute | solution.py:861
  185.2 19.5 %collective-permute-start.39 = (bf16[2,4,96,768]{3,2,1,0:T(8,128)(2,1)}, bf16[2,4,96,768]{3,2,1,0:T(8,128)(2,1)}, u32[]{:S(2)}, u32[]{:S(2)}) collective-permute-start(bf16[2,4,96,768]{3,2,1,0:T(8,128)(2,1)} %get-tuple-element.176), channel_id=1, source_target_pairs={{0,8},{1,17},{2,10},{3,19},{4,12},{5,21},{6,14},{7,23},{8,0},{9,25... | collective-permute-start | bytes 3538952 | tf_op jit(solution)/shard_map/ppermute | solution.py:873
  192.0 22.5 %collective-permute-start.40 = (bf16[2,4,96,768]{3,2,1,0:T(8,128)(2,1)}, bf16[2,4,96,768]{3,2,1,0:T(8,128)(2,1)}, u32[]{:S(2)}, u32[]{:S(2)}) collective-permute-start(bf16[2,4,96,768]{3,2,1,0:T(8,128)(2,1)} %get-tuple-element.177), channel_id=1, source_target_pairs={{0,8},{1,17},{2,10},{3,19},{4,12},{5,21},{6,14},{7,23},{8,0},{9,25... | collective-permute-start | bytes 3538952 | tf_op jit(solution)/shard_map/ppermute | solution.py:873
  193.3 25.5 %collective-permute-start.41 = (bf16[512,2304]{1,0:T(8,128)(2,1)}, bf16[512,2304]{1,0:T(8,128)(2,1)}, u32[]{:S(2)}, u32[]{:S(2)}) collective-permute-start(bf16[512,2304]{1,0:T(8,128)(2,1)} %get-tuple-element.180.refs_0_.refs_2_), channel_id=1, source_target_pairs={{0,1},{1,0},{2,3},{3,2},{4,5},{5,4},{6,7},{7,6},{8,9},{9,8},{10,11... | collective-permute-start | bytes 7077896 | tf_op jit(solution)/shard_map/ppermute | solution.py:861
  217.7 9.9 %collective-permute-start.42 = (bf16[256,3072]{1,0:T(8,128)(2,1)}, bf16[256,3072]{1,0:T(8,128)(2,1)}, u32[]{:S(2)}, u32[]{:S(2)}) collective-permute-start(bf16[256,3072]{1,0:T(8,128)(2,1)} %get-tuple-element.184.refs_2_.refs_0_), channel_id=1, source_target_pairs={{0,1},{1,0},{2,3},{3,2},{4,5},{5,4},{6,7},{7,6},{8,9},{9,8},{10,11... | collective-permute-start | bytes 4718600 | tf_op jit(solution)/shard_map/ppermute | solution.py:861
  217.7 21.3 %collective-permute-start.43 = (bf16[4,2,96,768]{3,2,1,0:T(8,128)(2,1)}, bf16[4,2,96,768]{3,2,1,0:T(8,128)(2,1)}, u32[]{:S(2)}, u32[]{:S(2)}) collective-permute-start(bf16[4,2,96,768]{3,2,1,0:T(8,128)(2,1)} %leaving.3), channel_id=1, source_target_pairs={{0,16},{1,9},{2,18},{3,11},{4,20},{5,13},{6,22},{7,15},{8,24},{9,1... | collective-permute-start | bytes 3538952 | tf_op jit(solution)/shard_map/ppermute | solution.py:879
  226.6 27.8 %collective-permute-start.44 = (bf16[2,4,96,768]{3,2,1,0:T(8,128)(2,1)}, bf16[2,4,96,768]{3,2,1,0:T(8,128)(2,1)}, u32[]{:S(2)}, u32[]{:S(2)}) collective-permute-start(bf16[2,4,96,768]{3,2,1,0:T(8,128)(2,1)} %get-tuple-element.191), channel_id=1, source_target_pairs={{0,8},{1,17},{2,10},{3,19},{4,12},{5,21},{6,14},{7,23},{8,0},{9,25... | collective-permute-start | bytes 3538952 | tf_op jit(solution)/shard_map/ppermute | solution.py:873
  233.5 30.8 %collective-permute-start.45 = (bf16[2,4,96,768]{3,2,1,0:T(8,128)(2,1)}, bf16[2,4,96,768]{3,2,1,0:T(8,128)(2,1)}, u32[]{:S(2)}, u32[]{:S(2)}) collective-permute-start(bf16[2,4,96,768]{3,2,1,0:T(8,128)(2,1)} %get-tuple-element.194), channel_id=1, source_target_pairs={{0,8},{1,17},{2,10},{3,19},{4,12},{5,21},{6,14},{7,23},{8,0},{9,25... | collective-permute-start | bytes 3538952 | tf_op jit(solution)/shard_map/ppermute | solution.py:873
  242.7 32.0 %all-to-all-start.4 = ((bf16[4,2,96,768]{3,2,1,0:T(8,128)(2,1)}), bf16[4,2,96,768]{3,2,1,0:T(8,128)(2,1)}, u32[]{:S(2)}, u32[]{:S(2)}) async-start(bf16[4,2,96,768]{3,2,1,0:T(8,128)(2,1)} %staying.2), calls=%async_computation.4 | async-start | bytes 2359296 | tf_op jit(solution)/shard_map/all_to_all | solution.py:888
  257.3 17.4 %collective-permute-start.46 = (bf16[4,96,768]{2,1,0:T(8,128)(2,1)}, bf16[4,96,768]{2,1,0:T(8,128)(2,1)S(1)}, u32[]{:S(2)}, u32[]{:S(2)}) collective-permute-start(bf16[4,96,768]{2,1,0:T(8,128)(2,1)} %leaving.4), channel_id=1, source_target_pairs={{0,16},{1,9},{2,18},{3,11},{4,20},{5,13},{6,22},{7,15},{8,24},{9,1... | collective-permute-start | bytes 1769480 | tf_op jit(solution)/shard_map/ppermute | solution.py:879
  267.4 10.3 %collective-permute-start.47 = (bf16[4,96,768]{2,1,0:T(8,128)(2,1)}, bf16[4,96,768]{2,1,0:T(8,128)(2,1)}, u32[]{:S(2)}, u32[]{:S(2)}) collective-permute-start(bf16[4,96,768]{2,1,0:T(8,128)(2,1)} %leaving.5), channel_id=1, source_target_pairs={{0,16},{1,9},{2,18},{3,11},{4,20},{5,13},{6,22},{7,15},{8,24},{9,1... | collective-permute-start | bytes 1769480 | tf_op jit(solution)/shard_map/ppermute | solution.py:879
  283.4 10.3 %collective-permute-start.55 = (bf16[2,9504]{1,0:T(2,128)(2,1)S(1)}, bf16[2,9504]{1,0:T(2,128)(2,1)S(1)}, u32[]{:S(2)}, u32[]{:S(2)}) collective-permute-start(bf16[2,9504]{1,0:T(2,128)(2,1)S(1)} %bitcast.127), channel_id=1, source_target_pairs={{0,6},{1,7},{2,0},{3,1},{4,2},{5,3},{6,4},{7,5},{8,14},{9,15},{10,... | collective-permute-start | bytes 114056 | tf_op jit(solution)/shard_map/ppermute | solution.py:865
  289.1 33.7 %all-to-all-start.5 = ((bf16[4,2,96,768]{3,2,1,0:T(8,128)(2,1)}), bf16[4,2,96,768]{3,2,1,0:T(8,128)(2,1)}, u32[]{:S(2)}, u32[]{:S(2)}) async-start(bf16[4,2,96,768]{3,2,1,0:T(8,128)(2,1)} %staying.3), calls=%async_computation.5 | async-start | bytes 2359296 | tf_op jit(solution)/shard_map/all_to_all | solution.py:888
  307.8 17.5 %collective-permute-start.51 = (bf16[2,2,96,768]{3,2,1,0:T(8,128)(2,1)S(1)}, bf16[2,2,96,768]{3,2,1,0:T(8,128)(2,1)S(1)}, u32[]{:S(2)}, u32[]{:S(2)}) collective-permute-start(bf16[2,2,96,768]{3,2,1,0:T(8,128)(2,1)S(1)} %pad_maximum_fusion.3), channel_id=1, source_target_pairs={{0,16},{1,9},{2,18},{3,11},{4,20},{5,13},{6,22},{7,15},{8,24},{9,1... | collective-permute-start | bytes 1769480 | tf_op jit(solution)/shard_map/ppermute | solution.py:879
  309.3 10.8 %collective-permute-start.61 = (f32[8,128]{1,0:T(8,128)S(1)}, f32[8,128]{1,0:T(8,128)S(1)}, u32[]{:S(2)}, u32[]{:S(2)}) collective-permute-start(f32[8,128]{1,0:T(8,128)S(1)} %add.186), channel_id=1, source_target_pairs={{0,6},{1,7},{2,0},{3,1},{4,2},{5,3},{6,4},{7,5},{8,14},{9,15},{10,... | collective-permute-start | bytes 12296 | tf_op jit(solution)/shard_map/ppermute | solution.py:865
  331.2 9.9 %collective-permute-start.49 = (bf16[2,2,96,768]{3,2,1,0:T(8,128)(2,1)S(1)}, bf16[2,2,96,768]{3,2,1,0:T(8,128)(2,1)S(1)}, u32[]{:S(2)}, u32[]{:S(2)}) collective-permute-start(bf16[2,2,96,768]{3,2,1,0:T(8,128)(2,1)S(1)} %pad_maximum_fusion.2), channel_id=1, source_target_pairs={{0,16},{1,9},{2,18},{3,11},{4,20},{5,13},{6,22},{7,15},{8,24},{9,1... | collective-permute-start | bytes 1769480 | tf_op jit(solution)/shard_map/ppermute | solution.py:879
  (69 other events, 396.7 us)
where the time goes:
time: 349 us; the launch traced here: 344 us
  Pallas kernels  142 us (41%)
  waiting for transfers between devices  77.1 us (22%)
  starting transfers between devices  74.5 us (21%)
  local copies, waits for them, and re-layouts  17.9 us (5%)
  other arithmetic  16.4 us (5%)
  matrix products  12.6 us (4%)
  between operations  3.67 us (1%)
    pallas_call x13, Pallas kernels, run(): pl.pallas_call(body, out_shape=[jax.ShapeDtypeStruct(shape, kind) for sha...  122 us
    all_to_all x6, starting transfers between devices, spread_z(): lax.all_to_all(values, 'fsdp', split_axis=0, concat_axis=0, tiled=True, a...  28.5 us
    ppermute x12, starting transfers between devices, turn_z(): lax.ppermute(values, BOTH, moves(lambda y, x, z, c: (y, x, (z + by) % 4,...  19.6 us
    pallas_call x5, Pallas kernels, combine(): pl.pallas_call(functools.partial(combine_kernel, [[index for _, index in...  16.2 us
    ppermute x6, waiting for transfers between devices, first_swap(): lax.ppermute(values, BOTH, moves(lambda y, x, z, c: (y, 1 - x, z, c) if c...  15.8 us
    ppermute x5, waiting for transfers between devices, swap_y(): lax.ppermute(values, BOTH, moves(lambda y, x, z, c: (1 - y, x, z, c)))  15.1 us
    ppermute x7, waiting for transfers between devices, second_swap(): lax.ppermute(values, BOTH, moves(lambda y, x, z, c: (1 - y, x, z, c) if c...  14.2 us
    all_to_all x6, waiting for transfers between devices, spread_z(): lax.all_to_all(values, 'fsdp', split_axis=0, concat_axis=0, tiled=True, a...  12 us
  transfers between devices with their start and end apart: 68, of which 27 were waited for; matrix products, arithmetic and copies ran while one was open for 11% of the time, Pallas kernels for 35%

commit v1 on v0

--- a/solution.py
+++ b/solution.py
@@ -1167,7 +1167,8 @@
     layer.ffn_in(w3)
     near_4 = [swap_x(column_4), swap_y(column_4)]
     got_3 = swap_core(layer.saved_3[1])
-    w4 = with_other([column_4] + near_4 + [far_4], layer.hidden)
+    near = [swap_core(after(part, layer.hidden)) for part in near_4]
+    w4 = [column_4] + near_4 + [far_4, swap_core(column_4)] + near + [swap_core(far_4)]
     layer.hold(got_3)
     layer.ffn_out(w4)
 
@@ -1190,22 +1191,23 @@
         return layer.block_grads(kernel, name, kept, got, grad, other, windows, rows)
 
     other = swap_core(layer.grad_branch)
+    layer.hold(other)
     layer.ffn_back(w4)
     other_pre = swap_core(layer.grad_pre)
-    layer.cross_back(w3, w2)
-    layer.hold(layer.cross_pack)
+    layer.hold(layer.grad_pre)
     g4 = grads(
         ffn_out_grad_kernel, "ffn_out_grad", layer.saved_3[0], got_3, layer.grad_branch, other
     )
-    s4 = first_way(g4)
-    other = swap_core(after(layer.cross_pack, g4[0]))
     layer.hold(g4[0])
     g3 = grads(
         ffn_in_grad_kernel, "ffn_in_grad", layer.saved_3[0], got_3, layer.grad_pre, other_pre
     )
-    s3 = first_way(g3)
+    s4, s3 = first_way(g4, g3[0]), first_way(g3)
     layer.hold(g3[0])
+    layer.cross_back(w3, w2)
+    layer.hold(layer.cross_pack)
     layer.self_back(w1, w2)
+    other = swap_core(after(layer.cross_pack, layer.self_pack))
     layer.hold(layer.self_pack)
     t43 = leaving(s4, s3)
     q43 = second_swap(t43)
@@ -1221,11 +1223,11 @@
     )
     s1 = first_way(g1)
     layer.hold(g1[0])
+    layer.token_back(w1)
+    layer.hold(layer.token_grad)
     u43 = staying(s4 + ((q43, (slice(None), 0)),), s3 + ((q43, (slice(None), 1)),))
     sent_43 = spread_z(u43)
     layer.hold(u43)
-    layer.token_back(w1)
-    layer.hold(layer.token_grad)
     t2 = leaving(s2)
     q2 = second_swap(t2)
     layer.hold(t2)
@@ -1233,12 +1235,12 @@
     layer.hold(layer.memory_grad)
     t1 = leaving(s1)
     q1 = second_swap(t1)
-    layer.hold(t1, sent_43)
-    own_4, own_3 = jnp.sum(after(sent_43, t1).astype(jnp.float32), axis=0)
+    layer.hold(t1)
     u21 = staying(s2 + (q2,), s1 + (q1,))
-    sent_21 = spread_z(u21)
-
-    pieces = after(layer.grad_generated().reshape(4, 2, -1), u21)
+    sent_21 = spread_z(after(u21, sent_43))
+    own_4, own_3 = jnp.sum(after(sent_43, u21).astype(jnp.float32), axis=0)
+
+    pieces = after(layer.grad_generated().reshape(4, 2, -1), u21, sent_43)
     mine = lax.dynamic_index_in_dim(pieces, c, 1, keepdims=False)
     theirs = lax.dynamic_index_in_dim(pieces, 1 - c, 1, keepdims=False)
     both = jnp.stack([mine, swap_core(theirs)], axis=1)

time: 349 us -> 340 us (0.974)
  waiting for transfers between devices: 77.1 us -> 71.5 us
    ppermute x6, waiting for transfers between devices: 15.8 us -> 10.4 us  [first_swap(): lax.ppermute(values, BOTH, moves(lambda y, x, z, c: (y, 1 - x, z, c) if c...]
    all_to_all x6, waiting for transfers between devices: 12 us -> 7.96 us  [spread_z(): lax.all_to_all(values, 'fsdp', split_axis=0, concat_axis=0, tiled=True, a...]
  transfers between devices with their start and end apart: 68 -> 68, of which waited for: 27 -> 26; matrix products, arithmetic and copies ran while one was open for 11% -> 11% of each run, Pallas kernels for 35% -> 35%
where the time goes in v1:
time: 340 us; the launch traced here: 337 us
  Pallas kernels  142 us (42%)
  starting transfers between devices  73.5 us (22%)
  waiting for transfers between devices  71.5 us (21%)
  local copies, waits for them, and re-layouts  16.9 us (5%)
  other arithmetic  16.3 us (5%)
  matrix products  12.4 us (4%)
  between operations  3.69 us (1%)
    pallas_call x13, Pallas kernels, run(): pl.pallas_call(body, out_shape=[jax.ShapeDtypeStruct(shape, kind) for sha...  123 us
    all_to_all x6, starting transfers between devices, spread_z(): lax.all_to_all(values, 'fsdp', split_axis=0, concat_axis=0, tiled=True, a...  28.3 us
    ppermute x12, starting transfers between devices, turn_z(): lax.ppermute(values, BOTH, moves(lambda y, x, z, c: (y, x, (z + by) % 4,...  19.7 us
    pallas_call x5, Pallas kernels, combine(): pl.pallas_call(functools.partial(combine_kernel, [[index for _, index in...  16.1 us
    ppermute x5, waiting for transfers between devices, swap_y(): lax.ppermute(values, BOTH, moves(lambda y, x, z, c: (1 - y, x, z, c)))  15.3 us
    ppermute x7, waiting for transfers between devices, second_swap(): lax.ppermute(values, BOTH, moves(lambda y, x, z, c: (1 - y, x, z, c) if c...  14.8 us
    ppermute x6, waiting for transfers between devices, first_swap(): lax.ppermute(values, BOTH, moves(lambda y, x, z, c: (y, 1 - x, z, c) if c...  10.4 us
    ppermute x27, waiting for transfers between devices, swap_core(): lax.ppermute(values, BOTH, moves(lambda y, x, z, c: (y, x, z, 1 - c)))  8.21 us
  transfers between devices with their start and end apart: 68, of which 26 were waited for; matrix products, arithmetic and copies ran while one was open for 11% of the time, Pallas kernels for 35%

profile of v1, /device:TPU:0, one launch (start us, length us, event | category | flops | bytes accessed | tf_op | source)
XLA Modules:
  0.0 336.7 jit_solution(9268817077229647766)
XLA Ops:
  1.3 3.6 %pick.1 = (bf16[4,96,768]{2,1,0:T(8,128)(2,1)}, bf16[4,96,768]{2,1,0:T(8,128)(2,1)}, bf16[4,2,96,768]{3,2,1,0:T(8,128)(2,1)}, bf16[4,2,96,768]{3,2,1,0:T(8,128)(2,1)}) custom-call(s32[3]{0:T(128)} %pad_add_fusion.scalars, bf16[96,2304]{1,0:T(8,128)(2,1)} %rest_0_.1, bf16[96,768]{1,0:T(8,128)(2,1)} %rest_1_.1, bf16[96,768]{1,0:T(8,128)(2,1)} %rest_2_.1, ...), custom_call_target="tpu_custom_call" | custom-call | flops 134217728 | bytes 131072 | tf_op jit(solution)/shard_map/pick/pallas_call | solution.py:648
  4.9 6.3 %all-to-all-start = ((bf16[4,96,768]{2,1,0:T(8,128)(2,1)}), bf16[4,96,768]{2,1,0:T(8,128)(2,1)S(1)}, u32[]{:S(2)}, u32[]{:S(2)}) async-start(bf16[4,96,768]{2,1,0:T(8,128)(2,1)} %get-tuple-element.112), calls=%async_computation | async-start | bytes 1179648 | tf_op jit(solution)/shard_map/all_to_all | solution.py:888
  30.3 3.5 %all-to-all-start.1 = ((bf16[4,96,768]{2,1,0:T(8,128)(2,1)}), bf16[4,96,768]{2,1,0:T(8,128)(2,1)S(1)}, u32[]{:S(2)}, u32[]{:S(2)}) async-start(bf16[4,96,768]{2,1,0:T(8,128)(2,1)} %get-tuple-element.114), calls=%async_computation.1 | async-start | bytes 1179648 | tf_op jit(solution)/shard_map/all_to_all | solution.py:888
  34.5 7.0 %collective-permute-done.5.refs_6_.refs_12_ = bf16[4,96,768]{2,1,0:T(8,128)(2,1)S(1)} collective-permute-done((bf16[4,96,768]{2,1,0:T(8,128)(2,1)S(1)}, bf16[4,96,768]{2,1,0:T(8,128)(2,1)S(1)}, u32[]{:S(2)}, u32[]{:S(2)}) %collective-permute-start.5) | collective-permute-done | bytes 589856 | tf_op jit(solution)/shard_map/ppermute | solution.py:857
  43.7 4.8 %all-to-all-done.1.refs_4_.refs_15_.refs_18_.refs_1_ = bf16[4,96,768]{2,1,0:T(8,128)(2,1)S(1)} async-done(((bf16[4,96,768]{2,1,0:T(8,128)(2,1)}), bf16[4,96,768]{2,1,0:T(8,128)(2,1)S(1)}, u32[]{:S(2)}, u32[]{:S(2)}) %all-to-all-start.1) | async-done | bytes 589856 | tf_op jit(solution)/shard_map/all_to_all | solution.py:888
  54.9 4.5 %all-to-all-start.2 = ((bf16[4,2,96,768]{3,2,1,0:T(8,128)(2,1)}), bf16[4,2,96,768]{3,2,1,0:T(8,128)(2,1)}, u32[]{:S(2)}, u32[]{:S(2)}) async-start(bf16[4,2,96,768]{3,2,1,0:T(8,128)(2,1)} %get-tuple-element.130), calls=%async_computation.2 | async-start | bytes 2359296 | tf_op jit(solution)/shard_map/all_to_all | solution.py:888
  68.4 10.8 %self_forward.1 = (bf16[256,2304]{1,0:T(8,128)(2,1)}, bf16[12,256,256]{2,1,0:T(8,128)(2,1)}, bf16[256,768]{1,0:T(8,128)(2,1)}, f32[256,24]{1,0:T(8,128)}, f32[25...) custom-call(s32[5]{0:T(128)} %concatenate.61.scalar_ref.scalars, ...), custom_call_target="tpu_custom_call" | custom-call | flops 2200000000 | bytes 2200000 | tf_op jit(solution)/shard_map/self_forward/pallas_call | solution.py:822
  89.0 4.3 %all-to-all-start.3 = ((bf16[4,2,96,768]{3,2,1,0:T(8,128)(2,1)}), bf16[4,2,96,768]{3,2,1,0:T(8,128)(2,1)}, u32[]{:S(2)}, u32[]{:S(2)}) async-start(bf16[4,2,96,768]{3,2,1,0:T(8,128)(2,1)} %get-tuple-element.143), calls=%async_computation.3 | async-start | bytes 2359296 | tf_op jit(solution)/shard_map/all_to_all | solution.py:888
  100.3 25.4 %cross_forward.1 = (bf16[256,768]{1,0:T(8,128)(2,1)}, bf16[512,1536]{1,0:T(8,128)(2,1)}, bf16[12,512,256]{2,1,0:T(8,128)(2,1)}, f32[256,768]{1,0:T(8,128)}, bf16...) custom-call(s32[5]{0:T(128)} %concatenate.61.scalar_ref.scalars, ...), custom_call_target="tpu_custom_call" | custom-call | flops 3000000000 | bytes 3000000 | tf_op jit(solution)/shard_map/cross_forward/pallas_call | solution.py:822
  131.8 8.7 %ffn_in.1 = (bf16[256,3072]{1,0:T(8,128)(2,1)}, bf16[256,3072]{1,0:T(8,128)(2,1)}, bf16[1920,256]{1,0:T(8,128)(2,1)}, bf16[1920,256]{1,0:T(8,128)(2,1)}) custom-call(s32[5]{0:T(128)} %concatenate.61.scalar_ref.scalars, bf16[256,768]{1,0:T(8,128)(2,1)} %get-tuple-element.138.refs_0_, bf16[4,96,768]{2,1,0:T(8,128)(2,1)} %slice_bitcast_fusion.3.refs_1_.refs_7_, ...), custom_call_target="tpu_custom_call" | custom-call | flops 1200000000 | bytes 1200000 | tf_op jit(solution)/shard_map/ffn_in/pallas_call | solution.py:822
  150.2 8.8 %ffn_out.1 = (bf16[256,768]{1,0:T(8,128)(2,1)}, bf16[256,768]{1,0:T(8,128)(2,1)}, f32[768,24]{1,0:T(8,128)}, f32[24,768]{1,0:T(8,128)}) custom-call(s32[5]{0:T(128)} %concatenate.61.scalar_ref.scalars, bf16[256,3072]{1,0:T(8,128)(2,1)} %get-tuple-element.152.refs_0_, f32[256,768]{1,0:T(8,128)} %get-tuple-element.153.refs_1_.refs_2_, ...), custom_call_target="tpu_custom_call" | custom-call | flops 1600000000 | bytes 1600000 | tf_op jit(solution)/shard_map/ffn_out/pallas_call | solution.py:822
  161.0 6.7 %ffn_back.1.refs_2_.refs_0_ = bf16[256,3072]{1,0:T(8,128)(2,1)} custom-call(s32[5]{0:T(128)} %concatenate.61.scalar_ref.scalars, bf16[256,768]{1,0:T(8,128)(2,1)} %get-tuple-element.157.refs_0_.refs_2_, bf16[256,3072]{1,0:T(8,128)(2,1)} %get-tuple-element.159.refs_1_, bf16[4,96,768]{2,1,0:T(8,128)(2,1)} %copy-done.3, ...), custom_call_target="tpu_custom_call" | custom-call | flops 1600000000 | bytes 1600000 | tf_op jit(solution)/shard_map/ffn_back/pallas_call | solution.py:822
  167.9 4.9 %ffn_out_grad.1 = (bf16[2,4,96,768]{3,2,1,0:T(8,128)(2,1)}, bf16[2,4,96,768]{3,2,1,0:T(8,128)(2,1)}) custom-call(s32[5]{0:T(128)} %concatenate.61.scalar_ref.scalars, bf16[1920,256]{1,0:T(8,128)(2,1)} %get-tuple-element.161.refs_0_, bf16[1920,256]{1,0:T(8,128)(2,1)} %copy-done.21, bf16[256,768]{1,0:T(8,128)(2,1)} %get-tuple-element.157.refs_0_.refs_2_, ...), custom_call_target="tpu_custom_call" | custom-call | flops 1000000000 | bytes 1000000 | tf_op jit(solution)/shard_map/ffn_out_grad/pallas_call | solution.py:822
  172.8 5.9 %ffn_in_grad.1 = (bf16[2,4,96,768]{3,2,1,0:T(8,128)(2,1)}, bf16[2,4,96,768]{3,2,1,0:T(8,128)(2,1)}) custom-call(s32[5]{0:T(128)} %concatenate.61.scalar_ref.scalars, bf16[1920,256]{1,0:T(8,128)(2,1)} %get-tuple-element.161.refs_0_, bf16[1920,256]{1,0:T(8,128)(2,1)} %copy-done.21, bf16[256,3072]{1,0:T(8,128)(2,1)} %ffn_back.1.refs_2_.refs_0_, ...), custom_call_target="tpu_custom_call" | custom-call | flops 1000000000 | bytes 1000000 | tf_op jit(solution)/shard_map/ffn_in_grad/pallas_call | solution.py:822
  180.9 14.4 %cross_back.1 = (f32[256,768]{1,0:T(8,128)}, f32[1,768]{1,0:T(1,128)}, bf16[512,2304]{1,0:T(8,128)(2,1)}) custom-call(s32[5]{0:T(128)} %concatenate.61.scalar_ref.scalars, bf16[256,3072]{1,0:T(8,128)(2,1)} %ffn_back.1.refs_2_.refs_0_, bf16[256,768]{1,0:T(8,128)(2,1)} %refs_1_.2, f32[256,768]{1,0:T(8,128)} %get-tuple-element.153.refs_1_.refs_2_, ...), custom_call_target="tpu_custom_call" | custom-call | flops 3000000000 | bytes 3000000 | tf_op jit(solution)/shard_map/cross_back/pallas_call | solution.py:822
  195.3 11.4 %self_back.1 = (f32[256,768]{1,0:T(8,128)}, f32[1,768]{1,0:T(1,128)}, f32[768,24]{1,0:T(8,128)}, f32[24,768]{1,0:T(8,128)}, bf16[256,3072]{1,0:T(8,128)(2,1)}) custom-call(s32[5]{0:T(128)} %concatenate.61.scalar_ref.scalars, bf16[512,2304]{1,0:T(8,128)(2,1)} %get-tuple-element.183.refs_0_.refs_2_, f32[256,768]{1,0:T(8,128)} %get-tuple-element.171.refs_1_, ...), custom_call_target="tpu_custom_call" | custom-call | flops 100000000 | bytes 100000 | tf_op jit(solution)/shard_map/self_back/pallas_call | solution.py:822
  212.4 7.8 %cross_grads.1 = (bf16[2,4,96,768]{3,2,1,0:T(8,128)(2,1)}, bf16[2,4,96,768]{3,2,1,0:T(8,128)(2,1)}) custom-call(s32[5]{0:T(128)} %concatenate.61.scalar_ref.scalars, bf16[1536,256]{1,0:T(8,128)(2,1)} %get-tuple-element.182.refs_0_, bf16[1536,256]{1,0:T(8,128)(2,1)} %copy-done.22, bf16[512,2304]{1,0:T(8,128)(2,1)} %get-tuple-element.183.refs_0_.refs_2_, ...), custom_call_target="tpu_custom_call" | custom-call | flops 1000000000 | bytes 1000000 | tf_op jit(solution)/shard_map/cross_grads/pallas_call | solution.py:822
  221.7 6.0 %self_grads.1 = (bf16[2,4,96,768]{3,2,1,0:T(8,128)(2,1)}, bf16[2,4,96,768]{3,2,1,0:T(8,128)(2,1)}) custom-call(s32[5]{0:T(128)} %concatenate.61.scalar_ref.scalars, bf16[768,256]{1,0:T(8,128)(2,1)} %get-tuple-element.186.refs_0_, bf16[768,256]{1,0:T(8,128)(2,1)} %copy-done.24, bf16[256,3072]{1,0:T(8,128)(2,1)} %get-tuple-element.187.refs_2_.refs_0_, ...), custom_call_target="tpu_custom_call" | custom-call | flops 1000000000 | bytes 1000000 | tf_op jit(solution)/shard_map/self_grads/pallas_call | solution.py:822
  228.4 6.3 %token_back.1 = (f32[256,768]{1,0:T(8,128)}, f32[1,768]{1,0:T(1,128)}) custom-call(s32[5]{0:T(128)} %concatenate.61.scalar_ref.scalars, bf16[256,3072]{1,0:T(8,128)(2,1)} %get-tuple-element.187.refs_2_.refs_0_, bf16[256,768]{1,0:T(8,128)(2,1)} %refs_1_.3, f32[256,768]{1,0:T(8,128)} %get-tuple-element.190.refs_2_, f32[3,768]{1,0:T(4,128)} %multiply_add_fusion.refs_1_.refs_3_, ...), custom_call_target="tpu_custom_call" | custom-call | flops 1000000000 | bytes 1000000 | tf_op jit(solution)/shard_map/token_back/pallas_call | solution.py:822
  234.7 3.6 %staying.2 = bf16[4,2,96,768]{3,2,1,0:T(8,128)(2,1)} custom-call(s32[5]{0:T(128)} %concatenate.61.scalar_ref.scalars, bf16[2,4,96,768]{3,2,1,0:T(8,128)(2,1)} %get-tuple-element.162.rest_0_, bf16[2,4,96,768]{3,2,1,0:T(8,128)(2,1)} %collective-permute-done.39.rest_1_, bf16[4,2,96,768]{3,2,1,0:T(8,128)(2,1)} %collective-permute-done.43.rest_2_.rest_5_, ...), custom_call_target="tpu_custom_call" | custom-call | flops 268435456 | bytes 262144 | tf_op jit(solution)/shard_map/staying/pallas_call | solution.py:582
  238.3 5.2 %all-to-all-start.4 = ((bf16[4,2,96,768]{3,2,1,0:T(8,128)(2,1)}), bf16[4,2,96,768]{3,2,1,0:T(8,128)(2,1)}, u32[]{:S(2)}, u32[]{:S(2)}) async-start(bf16[4,2,96,768]{3,2,1,0:T(8,128)(2,1)} %staying.2), calls=%async_computation.4 | async-start | bytes 2359296 | tf_op jit(solution)/shard_map/all_to_all | solution.py:888
  247.9 5.6 %memory_back.1 = f32[512,768]{1,0:T(8,128)} custom-call(s32[5]{0:T(128)} %concatenate.61.scalar_ref.scalars, bf16[512,2304]{1,0:T(8,128)(2,1)} %get-tuple-element.183.refs_0_.refs_2_, bf16[4,96,768]{2,1,0:T(8,128)(2,1)} %copy-done.2, bf16[4,96,768]{2,1,0:T(8,128)(2,1)} %collective-permute-done.15.refs_5_.refs_16_.refs_19_.refs_2_, ...), custom_call_target="tpu_custom_call" | custom-call | flops 60000000 | bytes 60000 | tf_op jit(solution)/shard_map/memory_back/pallas_call | solution.py:822
  262.7 7.4 %collective-permute-done.47.rest_5_ = bf16[4,96,768]{2,1,0:T(8,128)(2,1)} collective-permute-done((bf16[4,96,768]{2,1,0:T(8,128)(2,1)}, bf16[4,96,768]{2,1,0:T(8,128)(2,1)}, u32[]{:S(2)}, u32[]{:S(2)}) %collective-permute-start.47) | collective-permute-done | bytes 589856 | tf_op jit(solution)/shard_map/ppermute | solution.py:879
  270.1 3.6 %staying.3 = bf16[4,2,96,768]{3,2,1,0:T(8,128)(2,1)} custom-call(s32[5]{0:T(128)} %concatenate.61.scalar_ref.scalars, bf16[2,4,96,768]{3,2,1,0:T(8,128)(2,1)} %get-tuple-element.184.rest_0_, bf16[2,4,96,768]{3,2,1,0:T(8,128)(2,1)} %collective-permute-done.44.rest_1_, bf16[4,96,768]{2,1,0:T(8,128)(2,1)} %copy-done.23, ...), custom_call_target="tpu_custom_call" | custom-call | flops 268435456 | bytes 262144 | tf_op jit(solution)/shard_map/staying/pallas_call | solution.py:582
  275.8 3.9 %collective-permute-start.55 = (bf16[2,9504]{1,0:T(2,128)(2,1)S(1)}, bf16[2,9504]{1,0:T(2,128)(2,1)S(1)}, u32[]{:S(2)}, u32[]{:S(2)}) collective-permute-start(bf16[2,9504]{1,0:T(2,128)(2,1)S(1)} %bitcast.127), channel_id=1, source_target_pairs={{0,6},{1,7},{2,0},{3,1},{4,2},{5,3},{6,4},{7,5},{8,14},{9,15},{10,... | collective-permute-start | bytes 114056 | tf_op jit(solution)/shard_map/ppermute | solution.py:865
  281.5 4.6 %all-to-all-start.5 = ((bf16[4,2,96,768]{3,2,1,0:T(8,128)(2,1)}), bf16[4,2,96,768]{3,2,1,0:T(8,128)(2,1)}, u32[]{:S(2)}, u32[]{:S(2)}) async-start(bf16[4,2,96,768]{3,2,1,0:T(8,128)(2,1)} %staying.3), calls=%async_computation.5 | async-start | bytes 2359296 | tf_op jit(solution)/shard_map/all_to_all | solution.py:888
  288.1 3.6 %collective-permute-done.56 = bf16[8,9504]{1,0:T(8,128)(2,1)S(1)} collective-permute-done((bf16[8,9504]{1,0:T(8,128)(2,1)S(1)}, bf16[8,9504]{1,0:T(8,128)(2,1)S(1)}, u32[]{:S(2)}, u32[]{:S(2)}) %collective-permute-start.56) | collective-permute-done | bytes 152096 | tf_op jit(solution)/shard_map/ppermute | solution.py:853
  293.1 5.6 %collective-permute-done.57 = bf16[8,9504]{1,0:T(8,128)(2,1)S(1)} collective-permute-done((bf16[8,9504]{1,0:T(8,128)(2,1)S(1)}, bf16[8,9504]{1,0:T(8,128)(2,1)S(1)}, u32[]{:S(2)}, u32[]{:S(2)}) %collective-permute-start.57) | collective-permute-done | bytes 152096 | tf_op jit(solution)/shard_map/ppermute | solution.py:857
  301.7 3.8 %collective-permute-start.61 = (f32[8,128]{1,0:T(8,128)S(1)}, f32[8,128]{1,0:T(8,128)S(1)}, u32[]{:S(2)}, u32[]{:S(2)}) collective-permute-start(f32[8,128]{1,0:T(8,128)S(1)} %add.186), channel_id=1, source_target_pairs={{0,6},{1,7},{2,0},{3,1},{4,2},{5,3},{6,4},{7,5},{8,14},{9,15},{10,... | collective-permute-start | bytes 12296 | tf_op jit(solution)/shard_map/ppermute | solution.py:865
  306.6 5.7 %fusion = f32[128,9504]{0,1:T(8,128)} fusion(bf16[8,9504]{1,0:T(8,128)(2,1)S(1)} %collective-permute-done.57, bf16[8,9504]{1,0:T(8,128)(2,1)S(1)} %add_convert_fusion, f32[8,128]{1,0:T(8,128)S(1)} %fusion.62), kind=kOutput, calls=%fused_computation.32 | convolution fusion | flops 117022464 | bytes 5174272 | tf_op jit(solution)/shard_map/dot_general | solution.py:1334
  317.8 5.7 %collective-permute-done.48 = bf16[2,96,768]{2,1,0:T(8,128)(2,1)S(1)} collective-permute-done((bf16[2,96,768]{2,1,0:T(8,128)(2,1)S(1)}, bf16[2,96,768]{2,1,0:T(8,128)(2,1)S(1)}, u32[]{:S(2)}, u32[]{:S(2)}) %collective-permute-start.48) | collective-permute-done | bytes 294944 | tf_op jit(solution)/shard_map/ppermute | solution.py:873
  326.2 7.4 %collective-permute-done.49 = bf16[2,2,96,768]{3,2,1,0:T(8,128)(2,1)S(1)} collective-permute-done((bf16[2,2,96,768]{3,2,1,0:T(8,128)(2,1)S(1)}, bf16[2,2,96,768]{3,2,1,0:T(8,128)(2,1)S(1)}, u32[]{:S(2)}, u32[]{:S(2)}) %collective-permute-start.49) | collective-permute-done | bytes 589856 | tf_op jit(solution)/shard_map/ppermute | solution.py:879
  (257 shorter events, 116.1 us)
Async XLA Ops:
  4.9 22.3 %all-to-all-start = ((bf16[4,96,768]{2,1,0:T(8,128)(2,1)}), bf16[4,96,768]{2,1,0:T(8,128)(2,1)S(1)}, u32[]{:S(2)}, u32[]{:S(2)}) async-start(bf16[4,96,768]{2,1,0:T(8,128)(2,1)} %get-tuple-element.112), calls=%async_computation | async-start | bytes 1179648 | tf_op jit(solution)/shard_map/all_to_all | solution.py:888
  17.0 7.9 %collective-permute-start.3 = (s32[2,1]{0,1:T(1,128)S(1)}, s32[2,1]{0,1:T(1,128)S(1)}, u32[]{:S(2)}, u32[]{:S(2)}) collective-permute-start(s32[2,1]{0,1:T(1,128)S(1)} %pad_add_fusion.1), channel_id=1, source_target_pairs={{0,2},{1,3},{2,4},{3,5},{4,6},{5,7},{6,0},{7,1},{8,10},{9,11},{10,... | collective-permute-start | bytes 32 | tf_op jit(solution)/shard_map/ppermute | solution.py:865
  19.0 8.2 %collective-permute-start.2 = (s32[2,1]{0,1:T(1,128)S(1)}, s32[2,1]{0,1:T(1,128)S(1)}, u32[]{:S(2)}, u32[]{:S(2)}) collective-permute-start(s32[2,1]{0,1:T(1,128)S(1)} %pad_add_fusion.1), channel_id=1, source_target_pairs={{0,4},{1,5},{2,6},{3,7},{4,0},{5,1},{6,2},{7,3},{8,12},{9,13},{10,... | collective-permute-start | bytes 32 | tf_op jit(solution)/shard_map/ppermute | solution.py:865
  27.2 14.3 %collective-permute-start.5 = (bf16[4,96,768]{2,1,0:T(8,128)(2,1)S(1)}, bf16[4,96,768]{2,1,0:T(8,128)(2,1)S(1)}, u32[]{:S(2)}, u32[]{:S(2)}) collective-permute-start(bf16[4,96,768]{2,1,0:T(8,128)(2,1)S(1)} %all-to-all-done.refs_4_.refs_10_), channel_id=1, source_target_pairs={{0,16},{1,17},{2,18},{3,19},{4,20},{5,21},{6,22},{7,23},{8,24},{9,... | collective-permute-start | bytes 1769480 | tf_op jit(solution)/shard_map/ppermute | solution.py:857
  28.8 13.9 %collective-permute-start.4 = (bf16[4,96,768]{2,1,0:T(8,128)(2,1)S(1)}, bf16[4,96,768]{2,1,0:T(8,128)(2,1)S(1)}, u32[]{:S(2)}, u32[]{:S(2)}) collective-permute-start(bf16[4,96,768]{2,1,0:T(8,128)(2,1)S(1)} %all-to-all-done.refs_4_.refs_10_), channel_id=1, source_target_pairs={{0,8},{1,9},{2,10},{3,11},{4,12},{5,13},{6,14},{7,15},{8,0},{9,1},... | collective-permute-start | bytes 1769480 | tf_op jit(solution)/shard_map/ppermute | solution.py:853
  30.3 18.2 %all-to-all-start.1 = ((bf16[4,96,768]{2,1,0:T(8,128)(2,1)}), bf16[4,96,768]{2,1,0:T(8,128)(2,1)S(1)}, u32[]{:S(2)}, u32[]{:S(2)}) async-start(bf16[4,96,768]{2,1,0:T(8,128)(2,1)} %get-tuple-element.114), calls=%async_computation.1 | async-start | bytes 1179648 | tf_op jit(solution)/shard_map/all_to_all | solution.py:888
  52.6 11.3 %collective-permute-start.10 = (bf16[4,96,768]{2,1,0:T(8,128)(2,1)}, bf16[4,96,768]{2,1,0:T(8,128)(2,1)S(1)}, u32[]{:S(2)}, u32[]{:S(2)}) collective-permute-start(bf16[4,96,768]{2,1,0:T(8,128)(2,1)} %broadcast_select_fusion.1), channel_id=1, source_target_pairs={{0,16},{1,9},{2,18},{3,11},{4,20},{5,13},{6,22},{7,15},{8,24},{9,1... | collective-permute-start | bytes 1769480 | tf_op jit(solution)/shard_map/ppermute | solution.py:879
  53.2 11.5 %collective-permute-start.11 = (bf16[4,96,768]{2,1,0:T(8,128)(2,1)S(1)}, bf16[4,96,768]{2,1,0:T(8,128)(2,1)}, u32[]{:S(2)}, u32[]{:S(2)}) collective-permute-start(bf16[4,96,768]{2,1,0:T(8,128)(2,1)S(1)} %all-to-all-done.refs_4_.refs_10_), channel_id=1, source_target_pairs={{0,1},{1,0},{2,3},{3,2},{4,5},{5,4},{6,7},{7,6},{8,9},{9,8},{10,11... | collective-permute-start | bytes 1769480 | tf_op jit(solution)/shard_map/ppermute | solution.py:861
  54.9 32.1 %all-to-all-start.2 = ((bf16[4,2,96,768]{3,2,1,0:T(8,128)(2,1)}), bf16[4,2,96,768]{3,2,1,0:T(8,128)(2,1)}, u32[]{:S(2)}, u32[]{:S(2)}) async-start(bf16[4,2,96,768]{3,2,1,0:T(8,128)(2,1)} %get-tuple-element.130), calls=%async_computation.2 | async-start | bytes 2359296 | tf_op jit(solution)/shard_map/all_to_all | solution.py:888
  61.3 18.0 %collective-permute-start.16 = (bf16[4,96,768]{2,1,0:T(8,128)(2,1)S(1)}, bf16[4,96,768]{2,1,0:T(8,128)(2,1)}, u32[]{:S(2)}, u32[]{:S(2)}) collective-permute-start(bf16[4,96,768]{2,1,0:T(8,128)(2,1)S(1)} %all-to-all-done.1.refs_4_.refs_15_.refs_18_.refs_1_), channel_id=1, source_target_pairs={{0,16},{1,17},{2,18},{3,19},{4,20},{5,21},{6,22},{7,23},{8,24},{9,... | collective-permute-start | bytes 1769480 | tf_op jit(solution)/shard_map/ppermute | solution.py:857
  64.6 15.8 %collective-permute-start.15 = (bf16[4,96,768]{2,1,0:T(8,128)(2,1)S(1)}, bf16[4,96,768]{2,1,0:T(8,128)(2,1)}, u32[]{:S(2)}, u32[]{:S(2)}) collective-permute-start(bf16[4,96,768]{2,1,0:T(8,128)(2,1)S(1)} %all-to-all-done.1.refs_4_.refs_15_.refs_18_.refs_1_), channel_id=1, source_target_pairs={{0,8},{1,9},{2,10},{3,11},{4,12},{5,13},{6,14},{7,15},{8,0},{9,1},... | collective-permute-start | bytes 1769480 | tf_op jit(solution)/shard_map/ppermute | solution.py:853
  82.4 12.0 %collective-permute-start.18 = (bf16[4,96,768]{2,1,0:T(8,128)(2,1)}, bf16[4,96,768]{2,1,0:T(8,128)(2,1)S(1)}, u32[]{:S(2)}, u32[]{:S(2)}) collective-permute-start(bf16[4,96,768]{2,1,0:T(8,128)(2,1)} %broadcast_select_fusion), channel_id=1, source_target_pairs={{0,16},{1,9},{2,18},{3,11},{4,20},{5,13},{6,22},{7,15},{8,24},{9,1... | collective-permute-start | bytes 1769480 | tf_op jit(solution)/shard_map/ppermute | solution.py:879
  89.0 39.1 %all-to-all-start.3 = ((bf16[4,2,96,768]{3,2,1,0:T(8,128)(2,1)}), bf16[4,2,96,768]{3,2,1,0:T(8,128)(2,1)}, u32[]{:S(2)}, u32[]{:S(2)}) async-start(bf16[4,2,96,768]{3,2,1,0:T(8,128)(2,1)} %get-tuple-element.143), calls=%async_computation.3 | async-start | bytes 2359296 | tf_op jit(solution)/shard_map/all_to_all | solution.py:888
  96.1 29.6 %collective-permute-start.24 = (bf16[4,96,768]{2,1,0:T(8,128)(2,1)}, bf16[4,96,768]{2,1,0:T(8,128)(2,1)}, u32[]{:S(2)}, u32[]{:S(2)}) collective-permute-start(bf16[4,96,768]{2,1,0:T(8,128)(2,1)} %slice_bitcast_fusion.3.refs_1_.refs_7_), channel_id=1, source_target_pairs={{0,16},{1,17},{2,18},{3,19},{4,20},{5,21},{6,22},{7,23},{8,24},{9,... | collective-permute-start | bytes 1769480 | tf_op jit(solution)/shard_map/ppermute | solution.py:857
  97.6 28.1 %collective-permute-start.23 = (bf16[4,96,768]{2,1,0:T(8,128)(2,1)}, bf16[4,96,768]{2,1,0:T(8,128)(2,1)}, u32[]{:S(2)}, u32[]{:S(2)}) collective-permute-start(bf16[4,96,768]{2,1,0:T(8,128)(2,1)} %slice_bitcast_fusion.3.refs_1_.refs_7_), channel_id=1, source_target_pairs={{0,8},{1,9},{2,10},{3,11},{4,12},{5,13},{6,14},{7,15},{8,0},{9,1},... | collective-permute-start | bytes 1769480 | tf_op jit(solution)/shard_map/ppermute | solution.py:853
  129.2 15.8 %collective-permute-start.32 = (bf16[4,96,768]{2,1,0:T(8,128)(2,1)S(1)}, bf16[4,96,768]{2,1,0:T(8,128)(2,1)}, u32[]{:S(2)}, u32[]{:S(2)}) collective-permute-start(bf16[4,96,768]{2,1,0:T(8,128)(2,1)S(1)} %slice_bitcast_fusion.2.refs_5_.refs_2_), channel_id=1, source_target_pairs={{0,16},{1,17},{2,18},{3,19},{4,20},{5,21},{6,22},{7,23},{8,24},{9,... | collective-permute-start | bytes 1769480 | tf_op jit(solution)/shard_map/ppermute | solution.py:857
  130.9 15.5 %collective-permute-start.31 = (bf16[4,96,768]{2,1,0:T(8,128)(2,1)S(1)}, bf16[4,96,768]{2,1,0:T(8,128)(2,1)}, u32[]{:S(2)}, u32[]{:S(2)}) collective-permute-start(bf16[4,96,768]{2,1,0:T(8,128)(2,1)S(1)} %slice_bitcast_fusion.2.refs_5_.refs_2_), channel_id=1, source_target_pairs={{0,8},{1,9},{2,10},{3,11},{4,12},{5,13},{6,14},{7,15},{8,0},{9,1},... | collective-permute-start | bytes 1769480 | tf_op jit(solution)/shard_map/ppermute | solution.py:853
  178.8 28.0 %collective-permute-start.39 = (bf16[2,4,96,768]{3,2,1,0:T(8,128)(2,1)}, bf16[2,4,96,768]{3,2,1,0:T(8,128)(2,1)}, u32[]{:S(2)}, u32[]{:S(2)}) collective-permute-start(bf16[2,4,96,768]{3,2,1,0:T(8,128)(2,1)} %get-tuple-element.179), channel_id=1, source_target_pairs={{0,8},{1,17},{2,10},{3,19},{4,12},{5,21},{6,14},{7,23},{8,0},{9,25... | collective-permute-start | bytes 3538952 | tf_op jit(solution)/shard_map/ppermute | solution.py:873
  179.7 28.3 %collective-permute-start.40 = (bf16[2,4,96,768]{3,2,1,0:T(8,128)(2,1)}, bf16[2,4,96,768]{3,2,1,0:T(8,128)(2,1)}, u32[]{:S(2)}, u32[]{:S(2)}) collective-permute-start(bf16[2,4,96,768]{3,2,1,0:T(8,128)(2,1)} %get-tuple-element.180), channel_id=1, source_target_pairs={{0,8},{1,17},{2,10},{3,19},{4,12},{5,21},{6,14},{7,23},{8,0},{9,25... | collective-permute-start | bytes 3538952 | tf_op jit(solution)/shard_map/ppermute | solution.py:873
  211.2 10.5 %collective-permute-start.42 = (bf16[256,3072]{1,0:T(8,128)(2,1)}, bf16[256,3072]{1,0:T(8,128)(2,1)}, u32[]{:S(2)}, u32[]{:S(2)}) collective-permute-start(bf16[256,3072]{1,0:T(8,128)(2,1)} %get-tuple-element.187.refs_2_.refs_0_), channel_id=1, source_target_pairs={{0,1},{1,0},{2,3},{3,2},{4,5},{5,4},{6,7},{7,6},{8,9},{9,8},{10,11... | collective-permute-start | bytes 4718600 | tf_op jit(solution)/shard_map/ppermute | solution.py:861
  211.3 23.4 %collective-permute-start.43 = (bf16[4,2,96,768]{3,2,1,0:T(8,128)(2,1)}, bf16[4,2,96,768]{3,2,1,0:T(8,128)(2,1)}, u32[]{:S(2)}, u32[]{:S(2)}) collective-permute-start(bf16[4,2,96,768]{3,2,1,0:T(8,128)(2,1)} %leaving.3), channel_id=1, source_target_pairs={{0,16},{1,9},{2,18},{3,11},{4,20},{5,13},{6,22},{7,15},{8,24},{9,1... | collective-permute-start | bytes 3538952 | tf_op jit(solution)/shard_map/ppermute | solution.py:879
  220.2 23.3 %collective-permute-start.44 = (bf16[2,4,96,768]{3,2,1,0:T(8,128)(2,1)}, bf16[2,4,96,768]{3,2,1,0:T(8,128)(2,1)}, u32[]{:S(2)}, u32[]{:S(2)}) collective-permute-start(bf16[2,4,96,768]{3,2,1,0:T(8,128)(2,1)} %get-tuple-element.194), channel_id=1, source_target_pairs={{0,8},{1,17},{2,10},{3,19},{4,12},{5,21},{6,14},{7,23},{8,0},{9,25... | collective-permute-start | bytes 3538952 | tf_op jit(solution)/shard_map/ppermute | solution.py:873
  227.7 29.3 %collective-permute-start.45 = (bf16[2,4,96,768]{3,2,1,0:T(8,128)(2,1)}, bf16[2,4,96,768]{3,2,1,0:T(8,128)(2,1)}, u32[]{:S(2)}, u32[]{:S(2)}) collective-permute-start(bf16[2,4,96,768]{3,2,1,0:T(8,128)(2,1)} %get-tuple-element.197), channel_id=1, source_target_pairs={{0,8},{1,17},{2,10},{3,19},{4,12},{5,21},{6,14},{7,23},{8,0},{9,25... | collective-permute-start | bytes 3538952 | tf_op jit(solution)/shard_map/ppermute | solution.py:873
  238.3 35.4 %all-to-all-start.4 = ((bf16[4,2,96,768]{3,2,1,0:T(8,128)(2,1)}), bf16[4,2,96,768]{3,2,1,0:T(8,128)(2,1)}, u32[]{:S(2)}, u32[]{:S(2)}) async-start(bf16[4,2,96,768]{3,2,1,0:T(8,128)(2,1)} %staying.2), calls=%async_computation.4 | async-start | bytes 2359296 | tf_op jit(solution)/shard_map/all_to_all | solution.py:888
  246.3 16.3 %collective-permute-start.46 = (bf16[4,96,768]{2,1,0:T(8,128)(2,1)}, bf16[4,96,768]{2,1,0:T(8,128)(2,1)S(1)}, u32[]{:S(2)}, u32[]{:S(2)}) collective-permute-start(bf16[4,96,768]{2,1,0:T(8,128)(2,1)} %leaving.4), channel_id=1, source_target_pairs={{0,16},{1,9},{2,18},{3,11},{4,20},{5,13},{6,22},{7,15},{8,24},{9,1... | collective-permute-start | bytes 1769480 | tf_op jit(solution)/shard_map/ppermute | solution.py:879
  259.8 10.3 %collective-permute-start.47 = (bf16[4,96,768]{2,1,0:T(8,128)(2,1)}, bf16[4,96,768]{2,1,0:T(8,128)(2,1)}, u32[]{:S(2)}, u32[]{:S(2)}) collective-permute-start(bf16[4,96,768]{2,1,0:T(8,128)(2,1)} %leaving.5), channel_id=1, source_target_pairs={{0,16},{1,9},{2,18},{3,11},{4,20},{5,13},{6,22},{7,15},{8,24},{9,1... | collective-permute-start | bytes 1769480 | tf_op jit(solution)/shard_map/ppermute | solution.py:879
  275.8 10.3 %collective-permute-start.55 = (bf16[2,9504]{1,0:T(2,128)(2,1)S(1)}, bf16[2,9504]{1,0:T(2,128)(2,1)S(1)}, u32[]{:S(2)}, u32[]{:S(2)}) collective-permute-start(bf16[2,9504]{1,0:T(2,128)(2,1)S(1)} %bitcast.127), channel_id=1, source_target_pairs={{0,6},{1,7},{2,0},{3,1},{4,2},{5,3},{6,4},{7,5},{8,14},{9,15},{10,... | collective-permute-start | bytes 114056 | tf_op jit(solution)/shard_map/ppermute | solution.py:865
  281.5 33.7 %all-to-all-start.5 = ((bf16[4,2,96,768]{3,2,1,0:T(8,128)(2,1)}), bf16[4,2,96,768]{3,2,1,0:T(8,128)(2,1)}, u32[]{:S(2)}, u32[]{:S(2)}) async-start(bf16[4,2,96,768]{3,2,1,0:T(8,128)(2,1)} %staying.3), calls=%async_computation.5 | async-start | bytes 2359296 | tf_op jit(solution)/shard_map/all_to_all | solution.py:888
  300.0 17.7 %collective-permute-start.51 = (bf16[2,2,96,768]{3,2,1,0:T(8,128)(2,1)S(1)}, bf16[2,2,96,768]{3,2,1,0:T(8,128)(2,1)S(1)}, u32[]{:S(2)}, u32[]{:S(2)}) collective-permute-start(bf16[2,2,96,768]{3,2,1,0:T(8,128)(2,1)S(1)} %pad_maximum_fusion.3), channel_id=1, source_target_pairs={{0,16},{1,9},{2,18},{3,11},{4,20},{5,13},{6,22},{7,15},{8,24},{9,1... | collective-permute-start | bytes 1769480 | tf_op jit(solution)/shard_map/ppermute | solution.py:879
  301.7 10.6 %collective-permute-start.61 = (f32[8,128]{1,0:T(8,128)S(1)}, f32[8,128]{1,0:T(8,128)S(1)}, u32[]{:S(2)}, u32[]{:S(2)}) collective-permute-start(f32[8,128]{1,0:T(8,128)S(1)} %add.186), channel_id=1, source_target_pairs={{0,6},{1,7},{2,0},{3,1},{4,2},{5,3},{6,4},{7,5},{8,14},{9,15},{10,... | collective-permute-start | bytes 12296 | tf_op jit(solution)/shard_map/ppermute | solution.py:865
  305.5 9.0 %collective-permute-start.59 = (f32[8,128]{1,0:T(8,128)S(1)}, f32[8,128]{1,0:T(8,128)S(1)}, u32[]{:S(2)}, u32[]{:S(2)}) collective-permute-start(f32[8,128]{1,0:T(8,128)S(1)} %add.186), channel_id=1, source_target_pairs={{0,4},{1,5},{2,6},{3,7},{4,0},{5,1},{6,2},{7,3},{8,12},{9,13},{10,... | collective-permute-start | bytes 12296 | tf_op jit(solution)/shard_map/ppermute | solution.py:865
  323.6 9.9 %collective-permute-start.49 = (bf16[2,2,96,768]{3,2,1,0:T(8,128)(2,1)S(1)}, bf16[2,2,96,768]{3,2,1,0:T(8,128)(2,1)S(1)}, u32[]{:S(2)}, u32[]{:S(2)}) collective-permute-start(bf16[2,2,96,768]{3,2,1,0:T(8,128)(2,1)S(1)} %pad_maximum_fusion.2), channel_id=1, source_target_pairs={{0,16},{1,9},{2,18},{3,11},{4,20},{5,13},{6,22},{7,15},{8,24},{9,1... | collective-permute-start | bytes 1769480 | tf_op jit(solution)/shard_map/ppermute | solution.py:879
  (69 other events, 393.6 us)

commit v2 on v1

--- a/solution.py
+++ b/solution.py
@@ -204,6 +204,8 @@
 
 
 def pair_at(pair, base=0):
+    if isinstance(pair, int):
+        return slice(base + pair * 128, base + pair * 128 + 128)
     return pl.ds(pl.multiple_of(base + pair * 128, 128), 128)
 
 
@@ -211,14 +213,23 @@
     wide, low_spaces = spaces[:2], spaces[2:]
     pairs = HEADS // 2
     first(0, wide[0])
-
-    @pl.loop(0, pairs // 2)
-    def _(turn):
-        for i in range(2):
-            pair = turn * 2 + i
-            first(jnp.minimum(pair + 1, pairs - 1), wide[1 - i])
+    if wide[0].shape[1] > 256:
+        for pair in range(pairs):
+            i = pair % 2
+            if pair + 1 < pairs:
+                first(pair + 1, wide[1 - i])
             middle(pair, wide[i], low_spaces[i])
-            last(jnp.maximum(pair - 1, 0), low_spaces[1 - i])
+            if pair:
+                last(pair - 1, low_spaces[1 - i])
+    else:
+
+        @pl.loop(0, pairs // 2)
+        def _(turn):
+            for i in range(2):
+                pair = turn * 2 + i
+                first(jnp.minimum(pair + 1, pairs - 1), wide[1 - i])
+                middle(pair, wide[i], low_spaces[i])
+                last(jnp.maximum(pair - 1, 0), low_spaces[1 - i])
 
     last(pairs - 1, low_spaces[1])
 
@@ -1191,9 +1202,8 @@
         return layer.block_grads(kernel, name, kept, got, grad, other, windows, rows)
 
     other = swap_core(layer.grad_branch)
-    layer.hold(other)
     layer.ffn_back(w4)
-    other_pre = swap_core(layer.grad_pre)
+    other_pre = swap_core(after(layer.grad_pre, other))
     layer.hold(layer.grad_pre)
     g4 = grads(
         ffn_out_grad_kernel, "ffn_out_grad", layer.saved_3[0], got_3, layer.grad_branch, other

time: 340 us -> 339 us (level)
  transfers between devices with their start and end apart: 68 -> 68, of which waited for: 26 -> 26; matrix products, arithmetic and copies ran while one was open for 11% -> 11% of each run, Pallas kernels for 35% -> 36%
where the time goes in v2:
time: 339 us; the launch traced here: 335 us
  Pallas kernels  140 us (41%)
  starting transfers between devices  74.5 us (22%)
  waiting for transfers between devices  70.2 us (21%)
  local copies, waits for them, and re-layouts  17.4 us (5%)
  other arithmetic  16.5 us (5%)
  matrix products  12.4 us (4%)
  between operations  3.69 us (1%)
    pallas_call x13, Pallas kernels, run(): pl.pallas_call(body, out_shape=[jax.ShapeDtypeStruct(shape, kind) for sha...  121 us
    all_to_all x6, starting transfers between devices, spread_z(): lax.all_to_all(values, 'fsdp', split_axis=0, concat_axis=0, tiled=True, a...  28.3 us
    ppermute x12, starting transfers between devices, turn_z(): lax.ppermute(values, BOTH, moves(lambda y, x, z, c: (y, x, (z + by) % 4,...  19.7 us
    pallas_call x5, Pallas kernels, combine(): pl.pallas_call(functools.partial(combine_kernel, [[index for _, index in...  16.1 us
    ppermute x5, waiting for transfers between devices, swap_y(): lax.ppermute(values, BOTH, moves(lambda y, x, z, c: (1 - y, x, z, c)))  15.1 us
    ppermute x7, waiting for transfers between devices, second_swap(): lax.ppermute(values, BOTH, moves(lambda y, x, z, c: (1 - y, x, z, c) if c...  14 us
    ppermute x6, waiting for transfers between devices, first_swap(): lax.ppermute(values, BOTH, moves(lambda y, x, z, c: (y, 1 - x, z, c) if c...  12.1 us
    all_to_all x6, waiting for transfers between devices, spread_z(): lax.all_to_all(values, 'fsdp', split_axis=0, concat_axis=0, tiled=True, a...  8.02 us
  transfers between devices with their start and end apart: 68, of which 26 were waited for; matrix products, arithmetic and copies ran while one was open for 11% of the time, Pallas kernels for 36%

profile of v2, /device:TPU:0, one launch (start us, length us, event | category | flops | bytes accessed | tf_op | source)
XLA Modules:
  0.0 334.9 jit_solution(3682678800599961376)
XLA Ops:
  1.3 3.6 %pick.1 = (bf16[4,96,768]{2,1,0:T(8,128)(2,1)}, bf16[4,96,768]{2,1,0:T(8,128)(2,1)}, bf16[4,2,96,768]{3,2,1,0:T(8,128)(2,1)}, bf16[4,2,96,768]{3,2,1,0:T(8,128)(2,1)}) custom-call(s32[3]{0:T(128)} %pad_add_fusion.scalars, bf16[96,2304]{1,0:T(8,128)(2,1)} %rest_0_.1, bf16[96,768]{1,0:T(8,128)(2,1)} %rest_1_.1, bf16[96,768]{1,0:T(8,128)(2,1)} %rest_2_.1, ...), custom_call_target="tpu_custom_call" | custom-call | flops 134217728 | bytes 131072 | tf_op jit(solution)/shard_map/pick/pallas_call | solution.py:659
  4.9 6.3 %all-to-all-start = ((bf16[4,96,768]{2,1,0:T(8,128)(2,1)}), bf16[4,96,768]{2,1,0:T(8,128)(2,1)S(1)}, u32[]{:S(2)}, u32[]{:S(2)}) async-start(bf16[4,96,768]{2,1,0:T(8,128)(2,1)} %get-tuple-element.112), calls=%async_computation | async-start | bytes 1179648 | tf_op jit(solution)/shard_map/all_to_all | solution.py:899
  30.3 3.5 %all-to-all-start.1 = ((bf16[4,96,768]{2,1,0:T(8,128)(2,1)}), bf16[4,96,768]{2,1,0:T(8,128)(2,1)S(1)}, u32[]{:S(2)}, u32[]{:S(2)}) async-start(bf16[4,96,768]{2,1,0:T(8,128)(2,1)} %get-tuple-element.114), calls=%async_computation.1 | async-start | bytes 1179648 | tf_op jit(solution)/shard_map/all_to_all | solution.py:899
  34.5 7.0 %collective-permute-done.5.refs_6_.refs_12_ = bf16[4,96,768]{2,1,0:T(8,128)(2,1)S(1)} collective-permute-done((bf16[4,96,768]{2,1,0:T(8,128)(2,1)S(1)}, bf16[4,96,768]{2,1,0:T(8,128)(2,1)S(1)}, u32[]{:S(2)}, u32[]{:S(2)}) %collective-permute-start.5) | collective-permute-done | bytes 589856 | tf_op jit(solution)/shard_map/ppermute | solution.py:868
  43.7 4.8 %all-to-all-done.1.refs_4_.refs_15_.refs_18_.refs_1_ = bf16[4,96,768]{2,1,0:T(8,128)(2,1)S(1)} async-done(((bf16[4,96,768]{2,1,0:T(8,128)(2,1)}), bf16[4,96,768]{2,1,0:T(8,128)(2,1)S(1)}, u32[]{:S(2)}, u32[]{:S(2)}) %all-to-all-start.1) | async-done | bytes 589856 | tf_op jit(solution)/shard_map/all_to_all | solution.py:899
  54.9 4.5 %all-to-all-start.2 = ((bf16[4,2,96,768]{3,2,1,0:T(8,128)(2,1)}), bf16[4,2,96,768]{3,2,1,0:T(8,128)(2,1)}, u32[]{:S(2)}, u32[]{:S(2)}) async-start(bf16[4,2,96,768]{3,2,1,0:T(8,128)(2,1)} %get-tuple-element.130), calls=%async_computation.2 | async-start | bytes 2359296 | tf_op jit(solution)/shard_map/all_to_all | solution.py:899
  68.4 10.9 %self_forward.1 = (bf16[256,2304]{1,0:T(8,128)(2,1)}, bf16[12,256,256]{2,1,0:T(8,128)(2,1)}, bf16[256,768]{1,0:T(8,128)(2,1)}, f32[256,24]{1,0:T(8,128)}, f32[25...) custom-call(s32[5]{0:T(128)} %concatenate.61.scalar_ref.scalars, ...), custom_call_target="tpu_custom_call" | custom-call | flops 2200000000 | bytes 2200000 | tf_op jit(solution)/shard_map/self_forward/pallas_call | solution.py:833
  89.0 4.3 %all-to-all-start.3 = ((bf16[4,2,96,768]{3,2,1,0:T(8,128)(2,1)}), bf16[4,2,96,768]{3,2,1,0:T(8,128)(2,1)}, u32[]{:S(2)}, u32[]{:S(2)}) async-start(bf16[4,2,96,768]{3,2,1,0:T(8,128)(2,1)} %get-tuple-element.143), calls=%async_computation.3 | async-start | bytes 2359296 | tf_op jit(solution)/shard_map/all_to_all | solution.py:899
  100.3 24.7 %cross_forward.1 = (bf16[256,768]{1,0:T(8,128)(2,1)}, bf16[512,1536]{1,0:T(8,128)(2,1)}, bf16[12,512,256]{2,1,0:T(8,128)(2,1)}, f32[256,768]{1,0:T(8,128)}, bf16...) custom-call(s32[5]{0:T(128)} %concatenate.61.scalar_ref.scalars, ...), custom_call_target="tpu_custom_call" | custom-call | flops 3000000000 | bytes 3000000 | tf_op jit(solution)/shard_map/cross_forward/pallas_call | solution.py:833
  131.1 8.7 %ffn_in.1 = (bf16[256,3072]{1,0:T(8,128)(2,1)}, bf16[256,3072]{1,0:T(8,128)(2,1)}, bf16[1920,256]{1,0:T(8,128)(2,1)}, bf16[1920,256]{1,0:T(8,128)(2,1)}) custom-call(s32[5]{0:T(128)} %concatenate.61.scalar_ref.scalars, bf16[256,768]{1,0:T(8,128)(2,1)} %get-tuple-element.138.refs_0_, bf16[4,96,768]{2,1,0:T(8,128)(2,1)} %slice_bitcast_fusion.3.refs_1_.refs_7_, ...), custom_call_target="tpu_custom_call" | custom-call | flops 1200000000 | bytes 1200000 | tf_op jit(solution)/shard_map/ffn_in/pallas_call | solution.py:833
  149.5 8.8 %ffn_out.1 = (bf16[256,768]{1,0:T(8,128)(2,1)}, bf16[256,768]{1,0:T(8,128)(2,1)}, f32[768,24]{1,0:T(8,128)}, f32[24,768]{1,0:T(8,128)}) custom-call(s32[5]{0:T(128)} %concatenate.61.scalar_ref.scalars, bf16[256,3072]{1,0:T(8,128)(2,1)} %get-tuple-element.152.refs_0_, f32[256,768]{1,0:T(8,128)} %get-tuple-element.153.refs_1_.refs_2_, ...), custom_call_target="tpu_custom_call" | custom-call | flops 1600000000 | bytes 1600000 | tf_op jit(solution)/shard_map/ffn_out/pallas_call | solution.py:833
  158.6 6.7 %ffn_back.1.refs_2_.refs_0_ = bf16[256,3072]{1,0:T(8,128)(2,1)} custom-call(s32[5]{0:T(128)} %concatenate.61.scalar_ref.scalars, bf16[256,768]{1,0:T(8,128)(2,1)} %get-tuple-element.157.refs_0_.refs_2_, bf16[256,3072]{1,0:T(8,128)(2,1)} %get-tuple-element.158.refs_1_, bf16[4,96,768]{2,1,0:T(8,128)(2,1)} %copy-done.3, ...), custom_call_target="tpu_custom_call" | custom-call | flops 1600000000 | bytes 1600000 | tf_op jit(solution)/shard_map/ffn_back/pallas_call | solution.py:833
  166.0 4.9 %ffn_out_grad.1 = (bf16[2,4,96,768]{3,2,1,0:T(8,128)(2,1)}, bf16[2,4,96,768]{3,2,1,0:T(8,128)(2,1)}) custom-call(s32[5]{0:T(128)} %concatenate.61.scalar_ref.scalars, bf16[1920,256]{1,0:T(8,128)(2,1)} %get-tuple-element.160.refs_0_, bf16[1920,256]{1,0:T(8,128)(2,1)} %copy-done.21, bf16[256,768]{1,0:T(8,128)(2,1)} %get-tuple-element.157.refs_0_.refs_2_, ...), custom_call_target="tpu_custom_call" | custom-call | flops 1000000000 | bytes 1000000 | tf_op jit(solution)/shard_map/ffn_out_grad/pallas_call | solution.py:833
  170.9 5.9 %ffn_in_grad.1 = (bf16[2,4,96,768]{3,2,1,0:T(8,128)(2,1)}, bf16[2,4,96,768]{3,2,1,0:T(8,128)(2,1)}) custom-call(s32[5]{0:T(128)} %concatenate.61.scalar_ref.scalars, bf16[1920,256]{1,0:T(8,128)(2,1)} %get-tuple-element.160.refs_0_, bf16[1920,256]{1,0:T(8,128)(2,1)} %copy-done.21, bf16[256,3072]{1,0:T(8,128)(2,1)} %ffn_back.1.refs_2_.refs_0_, ...), custom_call_target="tpu_custom_call" | custom-call | flops 1000000000 | bytes 1000000 | tf_op jit(solution)/shard_map/ffn_in_grad/pallas_call | solution.py:833
  178.9 13.0 %cross_back.1 = (f32[256,768]{1,0:T(8,128)}, f32[1,768]{1,0:T(1,128)}, bf16[512,2304]{1,0:T(8,128)(2,1)}) custom-call(s32[5]{0:T(128)} %concatenate.61.scalar_ref.scalars, bf16[256,3072]{1,0:T(8,128)(2,1)} %ffn_back.1.refs_2_.refs_0_, bf16[256,768]{1,0:T(8,128)(2,1)} %refs_1_.2, f32[256,768]{1,0:T(8,128)} %get-tuple-element.153.refs_1_.refs_2_, ...), custom_call_target="tpu_custom_call" | custom-call | flops 3000000000 | bytes 3000000 | tf_op jit(solution)/shard_map/cross_back/pallas_call | solution.py:833
  191.9 11.4 %self_back.1 = (f32[256,768]{1,0:T(8,128)}, f32[1,768]{1,0:T(1,128)}, f32[768,24]{1,0:T(8,128)}, f32[24,768]{1,0:T(8,128)}, bf16[256,3072]{1,0:T(8,128)(2,1)}) custom-call(s32[5]{0:T(128)} %concatenate.61.scalar_ref.scalars, bf16[512,2304]{1,0:T(8,128)(2,1)} %get-tuple-element.183.refs_0_.refs_2_, f32[256,768]{1,0:T(8,128)} %get-tuple-element.171.refs_1_, ...), custom_call_target="tpu_custom_call" | custom-call | flops 100000000 | bytes 100000 | tf_op jit(solution)/shard_map/self_back/pallas_call | solution.py:833
  210.5 7.8 %cross_grads.1 = (bf16[2,4,96,768]{3,2,1,0:T(8,128)(2,1)}, bf16[2,4,96,768]{3,2,1,0:T(8,128)(2,1)}) custom-call(s32[5]{0:T(128)} %concatenate.61.scalar_ref.scalars, bf16[1536,256]{1,0:T(8,128)(2,1)} %get-tuple-element.182.refs_0_, bf16[1536,256]{1,0:T(8,128)(2,1)} %copy-done.22, bf16[512,2304]{1,0:T(8,128)(2,1)} %get-tuple-element.183.refs_0_.refs_2_, ...), custom_call_target="tpu_custom_call" | custom-call | flops 1000000000 | bytes 1000000 | tf_op jit(solution)/shard_map/cross_grads/pallas_call | solution.py:833
  219.2 6.0 %self_grads.1 = (bf16[2,4,96,768]{3,2,1,0:T(8,128)(2,1)}, bf16[2,4,96,768]{3,2,1,0:T(8,128)(2,1)}) custom-call(s32[5]{0:T(128)} %concatenate.61.scalar_ref.scalars, bf16[768,256]{1,0:T(8,128)(2,1)} %get-tuple-element.186.refs_0_, bf16[768,256]{1,0:T(8,128)(2,1)} %copy-done.24, bf16[256,3072]{1,0:T(8,128)(2,1)} %get-tuple-element.187.refs_2_.refs_0_, ...), custom_call_target="tpu_custom_call" | custom-call | flops 1000000000 | bytes 1000000 | tf_op jit(solution)/shard_map/self_grads/pallas_call | solution.py:833
  226.4 6.3 %token_back.1 = (f32[256,768]{1,0:T(8,128)}, f32[1,768]{1,0:T(1,128)}) custom-call(s32[5]{0:T(128)} %concatenate.61.scalar_ref.scalars, bf16[256,3072]{1,0:T(8,128)(2,1)} %get-tuple-element.187.refs_2_.refs_0_, bf16[256,768]{1,0:T(8,128)(2,1)} %refs_1_.3, f32[256,768]{1,0:T(8,128)} %get-tuple-element.190.refs_2_, f32[3,768]{1,0:T(4,128)} %multiply_add_fusion.refs_1_.refs_3_, ...), custom_call_target="tpu_custom_call" | custom-call | flops 1000000000 | bytes 1000000 | tf_op jit(solution)/shard_map/token_back/pallas_call | solution.py:833
  232.8 3.6 %staying.2 = bf16[4,2,96,768]{3,2,1,0:T(8,128)(2,1)} custom-call(s32[5]{0:T(128)} %concatenate.61.scalar_ref.scalars, bf16[2,4,96,768]{3,2,1,0:T(8,128)(2,1)} %get-tuple-element.161.rest_0_, bf16[2,4,96,768]{3,2,1,0:T(8,128)(2,1)} %collective-permute-done.39.rest_1_, bf16[4,2,96,768]{3,2,1,0:T(8,128)(2,1)} %collective-permute-done.43.rest_2_.rest_5_, ...), custom_call_target="tpu_custom_call" | custom-call | flops 268435456 | bytes 262144 | tf_op jit(solution)/shard_map/staying/pallas_call | solution.py:593
  236.4 5.2 %all-to-all-start.4 = ((bf16[4,2,96,768]{3,2,1,0:T(8,128)(2,1)}), bf16[4,2,96,768]{3,2,1,0:T(8,128)(2,1)}, u32[]{:S(2)}, u32[]{:S(2)}) async-start(bf16[4,2,96,768]{3,2,1,0:T(8,128)(2,1)} %staying.2), calls=%async_computation.4 | async-start | bytes 2359296 | tf_op jit(solution)/shard_map/all_to_all | solution.py:899
  246.0 5.6 %memory_back.1 = f32[512,768]{1,0:T(8,128)} custom-call(s32[5]{0:T(128)} %concatenate.61.scalar_ref.scalars, bf16[512,2304]{1,0:T(8,128)(2,1)} %get-tuple-element.183.refs_0_.refs_2_, bf16[4,96,768]{2,1,0:T(8,128)(2,1)} %copy-done.2, bf16[4,96,768]{2,1,0:T(8,128)(2,1)} %collective-permute-done.15.refs_5_.refs_16_.refs_19_.refs_2_, ...), custom_call_target="tpu_custom_call" | custom-call | flops 60000000 | bytes 60000 | tf_op jit(solution)/shard_map/memory_back/pallas_call | solution.py:833
  261.2 7.0 %collective-permute-done.47.rest_5_ = bf16[4,96,768]{2,1,0:T(8,128)(2,1)} collective-permute-done((bf16[4,96,768]{2,1,0:T(8,128)(2,1)}, bf16[4,96,768]{2,1,0:T(8,128)(2,1)}, u32[]{:S(2)}, u32[]{:S(2)}) %collective-permute-start.47) | collective-permute-done | bytes 589856 | tf_op jit(solution)/shard_map/ppermute | solution.py:890
  268.2 3.6 %staying.3 = bf16[4,2,96,768]{3,2,1,0:T(8,128)(2,1)} custom-call(s32[5]{0:T(128)} %concatenate.61.scalar_ref.scalars, bf16[2,4,96,768]{3,2,1,0:T(8,128)(2,1)} %get-tuple-element.184.rest_0_, bf16[2,4,96,768]{3,2,1,0:T(8,128)(2,1)} %collective-permute-done.44.rest_1_, bf16[4,96,768]{2,1,0:T(8,128)(2,1)} %copy-done.23, ...), custom_call_target="tpu_custom_call" | custom-call | flops 268435456 | bytes 262144 | tf_op jit(solution)/shard_map/staying/pallas_call | solution.py:593
  274.0 3.9 %collective-permute-start.55 = (bf16[2,9504]{1,0:T(2,128)(2,1)S(1)}, bf16[2,9504]{1,0:T(2,128)(2,1)S(1)}, u32[]{:S(2)}, u32[]{:S(2)}) collective-permute-start(bf16[2,9504]{1,0:T(2,128)(2,1)S(1)} %bitcast.127), channel_id=1, source_target_pairs={{0,6},{1,7},{2,0},{3,1},{4,2},{5,3},{6,4},{7,5},{8,14},{9,15},{10,... | collective-permute-start | bytes 114056 | tf_op jit(solution)/shard_map/ppermute | solution.py:876
  279.8 4.5 %all-to-all-start.5 = ((bf16[4,2,96,768]{3,2,1,0:T(8,128)(2,1)}), bf16[4,2,96,768]{3,2,1,0:T(8,128)(2,1)}, u32[]{:S(2)}, u32[]{:S(2)}) async-start(bf16[4,2,96,768]{3,2,1,0:T(8,128)(2,1)} %staying.3), calls=%async_computation.5 | async-start | bytes 2359296 | tf_op jit(solution)/shard_map/all_to_all | solution.py:899
  286.4 3.6 %collective-permute-done.56 = bf16[8,9504]{1,0:T(8,128)(2,1)S(1)} collective-permute-done((bf16[8,9504]{1,0:T(8,128)(2,1)S(1)}, bf16[8,9504]{1,0:T(8,128)(2,1)S(1)}, u32[]{:S(2)}, u32[]{:S(2)}) %collective-permute-start.56) | collective-permute-done | bytes 152096 | tf_op jit(solution)/shard_map/ppermute | solution.py:864
  291.5 5.5 %collective-permute-done.57 = bf16[8,9504]{1,0:T(8,128)(2,1)S(1)} collective-permute-done((bf16[8,9504]{1,0:T(8,128)(2,1)S(1)}, bf16[8,9504]{1,0:T(8,128)(2,1)S(1)}, u32[]{:S(2)}, u32[]{:S(2)}) %collective-permute-start.57) | collective-permute-done | bytes 152096 | tf_op jit(solution)/shard_map/ppermute | solution.py:868
  299.9 3.8 %collective-permute-start.61 = (f32[8,128]{1,0:T(8,128)S(1)}, f32[8,128]{1,0:T(8,128)S(1)}, u32[]{:S(2)}, u32[]{:S(2)}) collective-permute-start(f32[8,128]{1,0:T(8,128)S(1)} %add.186), channel_id=1, source_target_pairs={{0,6},{1,7},{2,0},{3,1},{4,2},{5,3},{6,4},{7,5},{8,14},{9,15},{10,... | collective-permute-start | bytes 12296 | tf_op jit(solution)/shard_map/ppermute | solution.py:876
  304.9 5.7 %fusion = f32[128,9504]{0,1:T(8,128)} fusion(bf16[8,9504]{1,0:T(8,128)(2,1)S(1)} %collective-permute-done.57, bf16[8,9504]{1,0:T(8,128)(2,1)S(1)} %add_convert_fusion, f32[8,128]{1,0:T(8,128)S(1)} %fusion.62), kind=kOutput, calls=%fused_computation.32 | convolution fusion | flops 117022464 | bytes 5174272 | tf_op jit(solution)/shard_map/dot_general | solution.py:1344
  316.1 5.7 %collective-permute-done.48 = bf16[2,96,768]{2,1,0:T(8,128)(2,1)S(1)} collective-permute-done((bf16[2,96,768]{2,1,0:T(8,128)(2,1)S(1)}, bf16[2,96,768]{2,1,0:T(8,128)(2,1)S(1)}, u32[]{:S(2)}, u32[]{:S(2)}) %collective-permute-start.48) | collective-permute-done | bytes 294944 | tf_op jit(solution)/shard_map/ppermute | solution.py:884
  324.8 7.0 %collective-permute-done.49 = bf16[2,2,96,768]{3,2,1,0:T(8,128)(2,1)S(1)} collective-permute-done((bf16[2,2,96,768]{3,2,1,0:T(8,128)(2,1)S(1)}, bf16[2,2,96,768]{3,2,1,0:T(8,128)(2,1)S(1)}, u32[]{:S(2)}, u32[]{:S(2)}) %collective-permute-start.49) | collective-permute-done | bytes 589856 | tf_op jit(solution)/shard_map/ppermute | solution.py:890
  (257 shorter events, 117.5 us)
Async XLA Ops:
  4.9 22.3 %all-to-all-start = ((bf16[4,96,768]{2,1,0:T(8,128)(2,1)}), bf16[4,96,768]{2,1,0:T(8,128)(2,1)S(1)}, u32[]{:S(2)}, u32[]{:S(2)}) async-start(bf16[4,96,768]{2,1,0:T(8,128)(2,1)} %get-tuple-element.112), calls=%async_computation | async-start | bytes 1179648 | tf_op jit(solution)/shard_map/all_to_all | solution.py:899
  17.2 7.7 %collective-permute-start.3 = (s32[2,1]{0,1:T(1,128)S(1)}, s32[2,1]{0,1:T(1,128)S(1)}, u32[]{:S(2)}, u32[]{:S(2)}) collective-permute-start(s32[2,1]{0,1:T(1,128)S(1)} %pad_add_fusion.1), channel_id=1, source_target_pairs={{0,2},{1,3},{2,4},{3,5},{4,6},{5,7},{6,0},{7,1},{8,10},{9,11},{10,... | collective-permute-start | bytes 32 | tf_op jit(solution)/shard_map/ppermute | solution.py:876
  19.2 8.0 %collective-permute-start.2 = (s32[2,1]{0,1:T(1,128)S(1)}, s32[2,1]{0,1:T(1,128)S(1)}, u32[]{:S(2)}, u32[]{:S(2)}) collective-permute-start(s32[2,1]{0,1:T(1,128)S(1)} %pad_add_fusion.1), channel_id=1, source_target_pairs={{0,4},{1,5},{2,6},{3,7},{4,0},{5,1},{6,2},{7,3},{8,12},{9,13},{10,... | collective-permute-start | bytes 32 | tf_op jit(solution)/shard_map/ppermute | solution.py:876
  27.2 14.3 %collective-permute-start.5 = (bf16[4,96,768]{2,1,0:T(8,128)(2,1)S(1)}, bf16[4,96,768]{2,1,0:T(8,128)(2,1)S(1)}, u32[]{:S(2)}, u32[]{:S(2)}) collective-permute-start(bf16[4,96,768]{2,1,0:T(8,128)(2,1)S(1)} %all-to-all-done.refs_4_.refs_10_), channel_id=1, source_target_pairs={{0,16},{1,17},{2,18},{3,19},{4,20},{5,21},{6,22},{7,23},{8,24},{9,... | collective-permute-start | bytes 1769480 | tf_op jit(solution)/shard_map/ppermute | solution.py:868
  28.8 13.9 %collective-permute-start.4 = (bf16[4,96,768]{2,1,0:T(8,128)(2,1)S(1)}, bf16[4,96,768]{2,1,0:T(8,128)(2,1)S(1)}, u32[]{:S(2)}, u32[]{:S(2)}) collective-permute-start(bf16[4,96,768]{2,1,0:T(8,128)(2,1)S(1)} %all-to-all-done.refs_4_.refs_10_), channel_id=1, source_target_pairs={{0,8},{1,9},{2,10},{3,11},{4,12},{5,13},{6,14},{7,15},{8,0},{9,1},... | collective-permute-start | bytes 1769480 | tf_op jit(solution)/shard_map/ppermute | solution.py:864
  30.3 18.2 %all-to-all-start.1 = ((bf16[4,96,768]{2,1,0:T(8,128)(2,1)}), bf16[4,96,768]{2,1,0:T(8,128)(2,1)S(1)}, u32[]{:S(2)}, u32[]{:S(2)}) async-start(bf16[4,96,768]{2,1,0:T(8,128)(2,1)} %get-tuple-element.114), calls=%async_computation.1 | async-start | bytes 1179648 | tf_op jit(solution)/shard_map/all_to_all | solution.py:899
  52.6 11.3 %collective-permute-start.10 = (bf16[4,96,768]{2,1,0:T(8,128)(2,1)}, bf16[4,96,768]{2,1,0:T(8,128)(2,1)S(1)}, u32[]{:S(2)}, u32[]{:S(2)}) collective-permute-start(bf16[4,96,768]{2,1,0:T(8,128)(2,1)} %broadcast_select_fusion.1), channel_id=1, source_target_pairs={{0,16},{1,9},{2,18},{3,11},{4,20},{5,13},{6,22},{7,15},{8,24},{9,1... | collective-permute-start | bytes 1769480 | tf_op jit(solution)/shard_map/ppermute | solution.py:890
  53.2 11.4 %collective-permute-start.11 = (bf16[4,96,768]{2,1,0:T(8,128)(2,1)S(1)}, bf16[4,96,768]{2,1,0:T(8,128)(2,1)}, u32[]{:S(2)}, u32[]{:S(2)}) collective-permute-start(bf16[4,96,768]{2,1,0:T(8,128)(2,1)S(1)} %all-to-all-done.refs_4_.refs_10_), channel_id=1, source_target_pairs={{0,1},{1,0},{2,3},{3,2},{4,5},{5,4},{6,7},{7,6},{8,9},{9,8},{10,11... | collective-permute-start | bytes 1769480 | tf_op jit(solution)/shard_map/ppermute | solution.py:872
  54.9 32.2 %all-to-all-start.2 = ((bf16[4,2,96,768]{3,2,1,0:T(8,128)(2,1)}), bf16[4,2,96,768]{3,2,1,0:T(8,128)(2,1)}, u32[]{:S(2)}, u32[]{:S(2)}) async-start(bf16[4,2,96,768]{3,2,1,0:T(8,128)(2,1)} %get-tuple-element.130), calls=%async_computation.2 | async-start | bytes 2359296 | tf_op jit(solution)/shard_map/all_to_all | solution.py:899
  61.3 18.0 %collective-permute-start.16 = (bf16[4,96,768]{2,1,0:T(8,128)(2,1)S(1)}, bf16[4,96,768]{2,1,0:T(8,128)(2,1)}, u32[]{:S(2)}, u32[]{:S(2)}) collective-permute-start(bf16[4,96,768]{2,1,0:T(8,128)(2,1)S(1)} %all-to-all-done.1.refs_4_.refs_15_.refs_18_.refs_1_), channel_id=1, source_target_pairs={{0,16},{1,17},{2,18},{3,19},{4,20},{5,21},{6,22},{7,23},{8,24},{9,... | collective-permute-start | bytes 1769480 | tf_op jit(solution)/shard_map/ppermute | solution.py:868
  64.6 15.8 %collective-permute-start.15 = (bf16[4,96,768]{2,1,0:T(8,128)(2,1)S(1)}, bf16[4,96,768]{2,1,0:T(8,128)(2,1)}, u32[]{:S(2)}, u32[]{:S(2)}) collective-permute-start(bf16[4,96,768]{2,1,0:T(8,128)(2,1)S(1)} %all-to-all-done.1.refs_4_.refs_15_.refs_18_.refs_1_), channel_id=1, source_target_pairs={{0,8},{1,9},{2,10},{3,11},{4,12},{5,13},{6,14},{7,15},{8,0},{9,1},... | collective-permute-start | bytes 1769480 | tf_op jit(solution)/shard_map/ppermute | solution.py:864
  82.3 12.0 %collective-permute-start.18 = (bf16[4,96,768]{2,1,0:T(8,128)(2,1)}, bf16[4,96,768]{2,1,0:T(8,128)(2,1)S(1)}, u32[]{:S(2)}, u32[]{:S(2)}) collective-permute-start(bf16[4,96,768]{2,1,0:T(8,128)(2,1)} %broadcast_select_fusion), channel_id=1, source_target_pairs={{0,16},{1,9},{2,18},{3,11},{4,20},{5,13},{6,22},{7,15},{8,24},{9,1... | collective-permute-start | bytes 1769480 | tf_op jit(solution)/shard_map/ppermute | solution.py:890
  89.0 38.4 %all-to-all-start.3 = ((bf16[4,2,96,768]{3,2,1,0:T(8,128)(2,1)}), bf16[4,2,96,768]{3,2,1,0:T(8,128)(2,1)}, u32[]{:S(2)}, u32[]{:S(2)}) async-start(bf16[4,2,96,768]{3,2,1,0:T(8,128)(2,1)} %get-tuple-element.143), calls=%async_computation.3 | async-start | bytes 2359296 | tf_op jit(solution)/shard_map/all_to_all | solution.py:899
  96.1 28.8 %collective-permute-start.24 = (bf16[4,96,768]{2,1,0:T(8,128)(2,1)}, bf16[4,96,768]{2,1,0:T(8,128)(2,1)}, u32[]{:S(2)}, u32[]{:S(2)}) collective-permute-start(bf16[4,96,768]{2,1,0:T(8,128)(2,1)} %slice_bitcast_fusion.3.refs_1_.refs_7_), channel_id=1, source_target_pairs={{0,16},{1,17},{2,18},{3,19},{4,20},{5,21},{6,22},{7,23},{8,24},{9,... | collective-permute-start | bytes 1769480 | tf_op jit(solution)/shard_map/ppermute | solution.py:868
  97.6 27.3 %collective-permute-start.23 = (bf16[4,96,768]{2,1,0:T(8,128)(2,1)}, bf16[4,96,768]{2,1,0:T(8,128)(2,1)}, u32[]{:S(2)}, u32[]{:S(2)}) collective-permute-start(bf16[4,96,768]{2,1,0:T(8,128)(2,1)} %slice_bitcast_fusion.3.refs_1_.refs_7_), channel_id=1, source_target_pairs={{0,8},{1,9},{2,10},{3,11},{4,12},{5,13},{6,14},{7,15},{8,0},{9,1},... | collective-permute-start | bytes 1769480 | tf_op jit(solution)/shard_map/ppermute | solution.py:864
  128.5 15.8 %collective-permute-start.32 = (bf16[4,96,768]{2,1,0:T(8,128)(2,1)S(1)}, bf16[4,96,768]{2,1,0:T(8,128)(2,1)}, u32[]{:S(2)}, u32[]{:S(2)}) collective-permute-start(bf16[4,96,768]{2,1,0:T(8,128)(2,1)S(1)} %slice_bitcast_fusion.2.refs_5_.refs_2_), channel_id=1, source_target_pairs={{0,16},{1,17},{2,18},{3,19},{4,20},{5,21},{6,22},{7,23},{8,24},{9,... | collective-permute-start | bytes 1769480 | tf_op jit(solution)/shard_map/ppermute | solution.py:868
  130.2 15.5 %collective-permute-start.31 = (bf16[4,96,768]{2,1,0:T(8,128)(2,1)S(1)}, bf16[4,96,768]{2,1,0:T(8,128)(2,1)}, u32[]{:S(2)}, u32[]{:S(2)}) collective-permute-start(bf16[4,96,768]{2,1,0:T(8,128)(2,1)S(1)} %slice_bitcast_fusion.2.refs_5_.refs_2_), channel_id=1, source_target_pairs={{0,8},{1,9},{2,10},{3,11},{4,12},{5,13},{6,14},{7,15},{8,0},{9,1},... | collective-permute-start | bytes 1769480 | tf_op jit(solution)/shard_map/ppermute | solution.py:864
  176.8 26.5 %collective-permute-start.39 = (bf16[2,4,96,768]{3,2,1,0:T(8,128)(2,1)}, bf16[2,4,96,768]{3,2,1,0:T(8,128)(2,1)}, u32[]{:S(2)}, u32[]{:S(2)}) collective-permute-start(bf16[2,4,96,768]{3,2,1,0:T(8,128)(2,1)} %get-tuple-element.179), channel_id=1, source_target_pairs={{0,8},{1,17},{2,10},{3,19},{4,12},{5,21},{6,14},{7,23},{8,0},{9,25... | collective-permute-start | bytes 3538952 | tf_op jit(solution)/shard_map/ppermute | solution.py:884
  177.8 28.3 %collective-permute-start.40 = (bf16[2,4,96,768]{3,2,1,0:T(8,128)(2,1)}, bf16[2,4,96,768]{3,2,1,0:T(8,128)(2,1)}, u32[]{:S(2)}, u32[]{:S(2)}) collective-permute-start(bf16[2,4,96,768]{3,2,1,0:T(8,128)(2,1)} %get-tuple-element.180), channel_id=1, source_target_pairs={{0,8},{1,17},{2,10},{3,19},{4,12},{5,21},{6,14},{7,23},{8,0},{9,25... | collective-permute-start | bytes 3538952 | tf_op jit(solution)/shard_map/ppermute | solution.py:884
  209.3 10.0 %collective-permute-start.42 = (bf16[256,3072]{1,0:T(8,128)(2,1)}, bf16[256,3072]{1,0:T(8,128)(2,1)}, u32[]{:S(2)}, u32[]{:S(2)}) collective-permute-start(bf16[256,3072]{1,0:T(8,128)(2,1)} %get-tuple-element.187.refs_2_.refs_0_), channel_id=1, source_target_pairs={{0,1},{1,0},{2,3},{3,2},{4,5},{5,4},{6,7},{7,6},{8,9},{9,8},{10,11... | collective-permute-start | bytes 4718600 | tf_op jit(solution)/shard_map/ppermute | solution.py:872
  209.4 23.4 %collective-permute-start.43 = (bf16[4,2,96,768]{3,2,1,0:T(8,128)(2,1)}, bf16[4,2,96,768]{3,2,1,0:T(8,128)(2,1)}, u32[]{:S(2)}, u32[]{:S(2)}) collective-permute-start(bf16[4,2,96,768]{3,2,1,0:T(8,128)(2,1)} %leaving.3), channel_id=1, source_target_pairs={{0,16},{1,9},{2,18},{3,11},{4,20},{5,13},{6,22},{7,15},{8,24},{9,1... | collective-permute-start | bytes 3538952 | tf_op jit(solution)/shard_map/ppermute | solution.py:890
  218.3 23.2 %collective-permute-start.44 = (bf16[2,4,96,768]{3,2,1,0:T(8,128)(2,1)}, bf16[2,4,96,768]{3,2,1,0:T(8,128)(2,1)}, u32[]{:S(2)}, u32[]{:S(2)}) collective-permute-start(bf16[2,4,96,768]{3,2,1,0:T(8,128)(2,1)} %get-tuple-element.194), channel_id=1, source_target_pairs={{0,8},{1,17},{2,10},{3,19},{4,12},{5,21},{6,14},{7,23},{8,0},{9,25... | collective-permute-start | bytes 3538952 | tf_op jit(solution)/shard_map/ppermute | solution.py:884
  225.2 29.8 %collective-permute-start.45 = (bf16[2,4,96,768]{3,2,1,0:T(8,128)(2,1)}, bf16[2,4,96,768]{3,2,1,0:T(8,128)(2,1)}, u32[]{:S(2)}, u32[]{:S(2)}) collective-permute-start(bf16[2,4,96,768]{3,2,1,0:T(8,128)(2,1)} %get-tuple-element.197), channel_id=1, source_target_pairs={{0,8},{1,17},{2,10},{3,19},{4,12},{5,21},{6,14},{7,23},{8,0},{9,25... | collective-permute-start | bytes 3538952 | tf_op jit(solution)/shard_map/ppermute | solution.py:884
  236.4 35.4 %all-to-all-start.4 = ((bf16[4,2,96,768]{3,2,1,0:T(8,128)(2,1)}), bf16[4,2,96,768]{3,2,1,0:T(8,128)(2,1)}, u32[]{:S(2)}, u32[]{:S(2)}) async-start(bf16[4,2,96,768]{3,2,1,0:T(8,128)(2,1)} %staying.2), calls=%async_computation.4 | async-start | bytes 2359296 | tf_op jit(solution)/shard_map/all_to_all | solution.py:899
  244.4 16.8 %collective-permute-start.46 = (bf16[4,96,768]{2,1,0:T(8,128)(2,1)}, bf16[4,96,768]{2,1,0:T(8,128)(2,1)S(1)}, u32[]{:S(2)}, u32[]{:S(2)}) collective-permute-start(bf16[4,96,768]{2,1,0:T(8,128)(2,1)} %leaving.4), channel_id=1, source_target_pairs={{0,16},{1,9},{2,18},{3,11},{4,20},{5,13},{6,22},{7,15},{8,24},{9,1... | collective-permute-start | bytes 1769480 | tf_op jit(solution)/shard_map/ppermute | solution.py:890
  257.9 10.3 %collective-permute-start.47 = (bf16[4,96,768]{2,1,0:T(8,128)(2,1)}, bf16[4,96,768]{2,1,0:T(8,128)(2,1)}, u32[]{:S(2)}, u32[]{:S(2)}) collective-permute-start(bf16[4,96,768]{2,1,0:T(8,128)(2,1)} %leaving.5), channel_id=1, source_target_pairs={{0,16},{1,9},{2,18},{3,11},{4,20},{5,13},{6,22},{7,15},{8,24},{9,1... | collective-permute-start | bytes 1769480 | tf_op jit(solution)/shard_map/ppermute | solution.py:890
  274.0 10.4 %collective-permute-start.55 = (bf16[2,9504]{1,0:T(2,128)(2,1)S(1)}, bf16[2,9504]{1,0:T(2,128)(2,1)S(1)}, u32[]{:S(2)}, u32[]{:S(2)}) collective-permute-start(bf16[2,9504]{1,0:T(2,128)(2,1)S(1)} %bitcast.127), channel_id=1, source_target_pairs={{0,6},{1,7},{2,0},{3,1},{4,2},{5,3},{6,4},{7,5},{8,14},{9,15},{10,... | collective-permute-start | bytes 114056 | tf_op jit(solution)/shard_map/ppermute | solution.py:876
  279.8 33.7 %all-to-all-start.5 = ((bf16[4,2,96,768]{3,2,1,0:T(8,128)(2,1)}), bf16[4,2,96,768]{3,2,1,0:T(8,128)(2,1)}, u32[]{:S(2)}, u32[]{:S(2)}) async-start(bf16[4,2,96,768]{3,2,1,0:T(8,128)(2,1)} %staying.3), calls=%async_computation.5 | async-start | bytes 2359296 | tf_op jit(solution)/shard_map/all_to_all | solution.py:899
  298.4 17.5 %collective-permute-start.51 = (bf16[2,2,96,768]{3,2,1,0:T(8,128)(2,1)S(1)}, bf16[2,2,96,768]{3,2,1,0:T(8,128)(2,1)S(1)}, u32[]{:S(2)}, u32[]{:S(2)}) collective-permute-start(bf16[2,2,96,768]{3,2,1,0:T(8,128)(2,1)S(1)} %pad_maximum_fusion.3), channel_id=1, source_target_pairs={{0,16},{1,9},{2,18},{3,11},{4,20},{5,13},{6,22},{7,15},{8,24},{9,1... | collective-permute-start | bytes 1769480 | tf_op jit(solution)/shard_map/ppermute | solution.py:890
  299.9 10.6 %collective-permute-start.61 = (f32[8,128]{1,0:T(8,128)S(1)}, f32[8,128]{1,0:T(8,128)S(1)}, u32[]{:S(2)}, u32[]{:S(2)}) collective-permute-start(f32[8,128]{1,0:T(8,128)S(1)} %add.186), channel_id=1, source_target_pairs={{0,6},{1,7},{2,0},{3,1},{4,2},{5,3},{6,4},{7,5},{8,14},{9,15},{10,... | collective-permute-start | bytes 12296 | tf_op jit(solution)/shard_map/ppermute | solution.py:876
  303.7 9.0 %collective-permute-start.59 = (f32[8,128]{1,0:T(8,128)S(1)}, f32[8,128]{1,0:T(8,128)S(1)}, u32[]{:S(2)}, u32[]{:S(2)}) collective-permute-start(f32[8,128]{1,0:T(8,128)S(1)} %add.186), channel_id=1, source_target_pairs={{0,4},{1,5},{2,6},{3,7},{4,0},{5,1},{6,2},{7,3},{8,12},{9,13},{10,... | collective-permute-start | bytes 12296 | tf_op jit(solution)/shard_map/ppermute | solution.py:876
  321.9 9.9 %collective-permute-start.49 = (bf16[2,2,96,768]{3,2,1,0:T(8,128)(2,1)S(1)}, bf16[2,2,96,768]{3,2,1,0:T(8,128)(2,1)S(1)}, u32[]{:S(2)}, u32[]{:S(2)}) collective-permute-start(bf16[2,2,96,768]{3,2,1,0:T(8,128)(2,1)S(1)} %pad_maximum_fusion.2), channel_id=1, source_target_pairs={{0,16},{1,9},{2,18},{3,11},{4,20},{5,13},{6,22},{7,15},{8,24},{9,1... | collective-permute-start | bytes 1769480 | tf_op jit(solution)/shard_map/ppermute | solution.py:890
  (69 other events, 396.5 us)
